TPU v7x, 32 devices: a whole 2x2x4 slice. The times are simulated.
32 devices in a mesh: dp: 4 (over z), seq: 2 (over core), expert: 4 (over y, x).
Axes of the slice: x: 2, y: 2, z: 4, core: 2. Of those that a mesh axis runs over, the one named last changes fastest.
Arguments:
- keys: bfloat16 [4, 1024, 512], P('expert', ('dp', 'seq')), may hold values from -4 to 4
- values: bfloat16 [4, 1024, 512], P('expert', ('dp', 'seq')), may hold values from -5 to 5
- queries: bfloat16 [4, 8, 4096], P('expert', ('dp', 'seq')), may hold values from -80 to 80
- residual: bfloat16 [4, 8, 2048], P('expert', ('dp', 'seq')), may hold values from -9 to 9
- out_proj: bfloat16 [4096, 2048], P(('dp', 'seq')), may hold values from -0.09375 to 0.09375
- norm_gain: bfloat16 [2048], replicated, may hold values from 0.25 to 1.75
- router: bfloat16 [2048, 16], replicated, may hold values from -8 to 8
- w_gate: bfloat16 [16, 2048, 768], P(('dp', 'expert'), None, 'seq'), may hold values from -0.125 to 0.125
- w_up: bfloat16 [16, 2048, 768], P(('dp', 'expert'), None, 'seq'), may hold values from -0.125 to 0.125
- w_down: bfloat16 [16, 768, 2048], P(('dp', 'expert'), 'seq'), may hold values from -0.21875 to 0.21875
- head_vec: bfloat16 [2048], replicated, may hold values from -0.09 to 0.09
- routes: int32 [4, 8, 8], P('expert', 'dp'), may hold values from 0 to 15, all different within a row; in each aligned block of 2 rows (0 to 1, 2 to 3, ..., all dimensions but the last counted through in order) at most 2 rows name the same one
- step_pos: int32 [4, 8], P('expert'), may hold values from 0 to 1023, as said below
- labels: int32 [4, 8], P('expert', ('dp', 'seq')), may hold values 0 or 1
- trace_len: int32 [4, 8], P('expert'), may hold values from 1 to 256, 1024 in all within a row
Outputs:
- loss: float32 [], replicated
- grad_down: bfloat16 [16, 768, 2048], P(('dp', 'expert'), 'seq')
- grad_router: bfloat16 [2048, 16], P(('dp', 'seq', 'expert'))
Inputs may be any that keep to these rules, and one draw needn't show every extreme that they name: `step_pos`: increasing along each pack; distinct. `routes`: in each aligned block of 2 step ends (those of one index of dp in one pack) no expert is named by more than 2 of them.
All inputs are finite; a program needn't handle non-finite values. No bound on the sum of `labels` on one device may be relied on, other than what follows from the above.
Results may differ from a plain program's by a relative error of at most 0.018.
Values may be sent and summed in bfloat16 or wider, within the bound.
A program may use at most 64 MiB of HBM per device.

v0:
```python
import jax
import jax.numpy as jnp
from jax import lax
from jax.sharding import PartitionSpec as P

QUERY_HEADS = 32
KEY_VALUE_HEADS = 4
HEAD_WIDTH = 128


MASKED = -1e30
EPSILON = 1e-06


def rms_scale(stream):
    return lax.rsqrt(jnp.mean(stream * stream, axis=-1, keepdims=True) + EPSILON)


def head_logit(final, head_vec):
    return jnp.sum(final * rms_scale(final) * head_vec.astype(jnp.float32)[None, :], axis=1)


def move_rows(buffer):
    return lax.all_to_all(buffer, ("dp", "expert"), split_axis=0, concat_axis=0, tiled=True)


def move_back(buffer):
    return lax.all_to_all(
        buffer.astype(jnp.bfloat16), ("dp", "expert"), split_axis=0, concat_axis=0, tiled=True
    ).astype(buffer.dtype)


def merge_heads(parts):
    weighted_r, totals_r, peak_r = parts
    peak_all = jnp.max(peak_r, axis=0)
    factor = jnp.exp(peak_r - peak_all[None])
    weighted_sum = jnp.sum(weighted_r * factor[..., None], axis=0)
    totals_sum = jnp.sum(totals_r * factor, axis=0)
    merged = weighted_sum / totals_sum[..., None]
    return merged.reshape(merged.shape[0], -1).astype(jnp.bfloat16)


def shards(
    keys,
    values,
    queries,
    residual,
    out_proj,
    norm_gain,
    router,
    w_gate,
    w_up,
    w_down,
    head_vec,
    routes,
    step_pos,
    labels,
    trace_len,
):
    count_of_keys = keys.shape[1]
    query_groups = QUERY_HEADS // KEY_VALUE_HEADS
    query_all = lax.all_gather(queries, ("dp", "seq"), axis=1, tiled=True)[0]
    positions = step_pos[0]
    number_of_steps = positions.shape[0]
    lengths = trace_len[0]
    trace_ends = jnp.cumsum(lengths)
    starts = jnp.sum(
        jnp.where(trace_ends[None, :] <= positions[:, None], lengths[None, :], 0), axis=1
    )
    key_pos = lax.axis_index(("dp", "seq")) * count_of_keys + jnp.arange(
        count_of_keys, dtype=jnp.int32
    )
    allowed = (key_pos[None, :] <= positions[:, None]) & (key_pos[None, :] >= starts[:, None])
    score_list = []
    for head_cluster in range(KEY_VALUE_HEADS):
        query_part = query_all[
            :,
            head_cluster
            * query_groups
            * HEAD_WIDTH : (head_cluster + 1)
            * query_groups
            * HEAD_WIDTH,
        ].reshape(number_of_steps * query_groups, HEAD_WIDTH)
        key_part = keys[0, :, head_cluster * HEAD_WIDTH : (head_cluster + 1) * HEAD_WIDTH]
        score_part = lax.dot_general(
            query_part, key_part, (((1,), (1,)), ((), ())), preferred_element_type=jnp.float32
        ) * HEAD_WIDTH ** (-0.5)
        score_part = score_part.reshape(number_of_steps, query_groups, count_of_keys)
        score_list.append(jnp.where(allowed[:, None, :], score_part, MASKED))
    scores = jnp.stack(score_list, axis=1).reshape(number_of_steps, QUERY_HEADS, count_of_keys)
    local_peak = jnp.max(scores, axis=2)
    heads_of_values = values[0].reshape(count_of_keys, KEY_VALUE_HEADS, HEAD_WIDTH)
    complete_weight_rows = jnp.where(
        allowed[:, None, :], jnp.exp(scores - local_peak[:, :, None]), 0.0
    )
    totals = jnp.sum(complete_weight_rows, axis=2)
    reduced_weight_rows = complete_weight_rows.astype(jnp.bfloat16).reshape(
        number_of_steps, KEY_VALUE_HEADS, query_groups, count_of_keys
    )
    weighted = jnp.einsum(
        "skgt,tkd->skgd", reduced_weight_rows, heads_of_values, preferred_element_type=jnp.float32
    )
    weighted, totals = (weighted.reshape(number_of_steps, QUERY_HEADS * HEAD_WIDTH), totals)
    attn = merge_heads(
        (
            lax.all_to_all(
                weighted.reshape(1, number_of_steps, QUERY_HEADS, HEAD_WIDTH).astype(jnp.bfloat16),
                ("dp", "seq"),
                split_axis=2,
                concat_axis=0,
                tiled=True,
            ).astype(jnp.float32),
            lax.all_to_all(
                totals.reshape(1, number_of_steps, QUERY_HEADS).astype(jnp.bfloat16),
                ("dp", "seq"),
                split_axis=2,
                concat_axis=0,
                tiled=True,
            ).astype(jnp.float32),
            lax.all_to_all(
                local_peak.reshape(1, number_of_steps, QUERY_HEADS).astype(jnp.bfloat16),
                ("dp", "seq"),
                split_axis=2,
                concat_axis=0,
                tiled=True,
            ).astype(jnp.float32),
        )
    )
    mixed = lax.psum_scatter(
        jnp.dot(attn, out_proj, preferred_element_type=jnp.float32).astype(jnp.bfloat16),
        ("dp", "seq"),
        scatter_dimension=0,
        tiled=True,
    ).astype(jnp.float32)
    stream = residual[0].astype(jnp.float32) + mixed
    normed = (stream * rms_scale(stream) * norm_gain.astype(jnp.float32)[None, :]).astype(
        jnp.bfloat16
    )
    block_normed = lax.all_gather(normed, "seq", axis=0, tiled=True)
    block_rows = routes.shape[1]
    topk = routes.shape[2]
    experts = router.shape[1]
    capacity = min(block_rows, 2 * ((block_rows * topk + experts - 1) // experts))
    route_ids = routes[0]
    logits = jnp.dot(block_normed, router, preferred_element_type=jnp.float32)
    chosen = (route_ids[:, :, None] == jnp.arange(experts, dtype=jnp.int32)[None, None, :]).astype(
        jnp.float32
    )
    picked = jnp.sum(chosen * logits[:, None, :], axis=2)
    gate_weight = jax.nn.softmax(picked, axis=-1)
    flat_routes = route_ids.reshape(-1)
    onehot = (flat_routes[:, None] == jnp.arange(experts, dtype=jnp.int32)[None, :]).astype(
        jnp.int32
    )
    order_rank = jnp.sum((jnp.cumsum(onehot, axis=0) - 1) * onehot, axis=1)
    slot_index = flat_routes * capacity + order_rank
    place_map = (
        slot_index[:, None] == jnp.arange(experts * capacity, dtype=jnp.int32)[None, :]
    ).astype(jnp.float32)
    place_map = place_map.reshape(block_rows, topk, experts * capacity)
    row_map = jnp.sum(place_map, axis=1)
    weight_map = jnp.sum(gate_weight[:, :, None] * place_map, axis=1)
    contract_rows = (((0,), (0,)), ((), ()))
    send_rows = lax.dot_general(
        row_map.astype(jnp.bfloat16),
        block_normed,
        contract_rows,
        preferred_element_type=jnp.float32,
    ).astype(jnp.bfloat16)
    arrived = move_rows(send_rows.reshape(experts, capacity, -1))
    width = arrived.shape[2]
    arrived = arrived.reshape(experts * capacity, width)
    gate_act = jnp.dot(arrived, w_gate[0], preferred_element_type=jnp.float32)
    up_act = jnp.dot(arrived, w_up[0], preferred_element_type=jnp.float32)
    hidden = (jax.nn.silu(gate_act) * up_act).astype(jnp.bfloat16)
    partial_value = jnp.dot(hidden, w_down[0], preferred_element_type=jnp.float32)
    returned = move_back(partial_value.reshape(experts, capacity, width)).reshape(
        experts * capacity, width
    )
    block_mix = lax.dot_general(
        weight_map, returned, (((1,), (0,)), ((), ())), precision=lax.Precision.HIGHEST
    )
    expert_mix = lax.psum_scatter(
        block_mix.astype(jnp.bfloat16), "seq", scatter_dimension=0, tiled=True
    ).astype(jnp.float32)
    final = stream + expert_mix
    reward, pull = jax.vjp(lambda value: head_logit(value, head_vec), final)
    target = labels[0].astype(jnp.float32)
    local_loss = jnp.sum(jax.nn.softplus(reward) - target * reward)
    loss = lax.psum(local_loss, ("dp", "seq", "expert"))
    logit_grad = jax.nn.sigmoid(reward) - target
    (final_grad,) = pull(logit_grad)
    d_mix = final_grad.astype(jnp.bfloat16)
    block_grads = lax.all_gather(d_mix, "seq", axis=0, tiled=True)
    slot_grads = lax.dot_general(
        row_map.astype(jnp.bfloat16), block_grads, contract_rows, preferred_element_type=jnp.float32
    )
    slot_dots = jnp.sum(slot_grads * returned, axis=1)
    dots_part = jnp.sum(place_map * slot_dots[None, None, :], axis=2)
    d_out = lax.dot_general(
        weight_map, block_grads.astype(jnp.float32), contract_rows, precision=lax.Precision.HIGHEST
    ).astype(jnp.bfloat16)
    grads_arrived = move_rows(d_out.reshape(experts, capacity, width)).reshape(
        experts * capacity, width
    )
    grad_down = lax.dot_general(
        hidden, grads_arrived, contract_rows, preferred_element_type=jnp.float32
    )
    grad_down = grad_down.astype(jnp.bfloat16).reshape((1,) + grad_down.shape)
    route_dot = lax.psum(dots_part, "seq")
    pick_grad = gate_weight * (route_dot - jnp.sum(gate_weight * route_dot, axis=1, keepdims=True))
    d_logits = jnp.sum(chosen * pick_grad[:, :, None], axis=1)
    columns = block_normed.reshape(
        block_rows, lax.axis_size("dp"), lax.axis_size("seq"), lax.axis_size("expert"), -1
    )
    my_columns = lax.dynamic_index_in_dim(
        columns, lax.axis_index("seq"), 2, keepdims=False
    ).reshape(block_rows, -1)
    router_part = lax.dot_general(
        my_columns.astype(jnp.float32), d_logits, contract_rows, precision=lax.Precision.HIGHEST
    )
    grad_router = lax.psum_scatter(
        router_part, ("dp", "expert"), scatter_dimension=0, tiled=True
    ).astype(jnp.bfloat16)
    return (loss, grad_down, grad_router)


def solution(mesh):
    return jax.shard_map(
        shards,
        mesh=mesh,
        in_specs=(
            P("expert", ("dp", "seq"), None),
            P("expert", ("dp", "seq"), None),
            P("expert", ("dp", "seq"), None),
            P("expert", ("dp", "seq"), None),
            P(("dp", "seq"), None),
            P(),
            P(),
            P(("dp", "expert"), None, "seq"),
            P(("dp", "expert"), None, "seq"),
            P(("dp", "expert"), "seq", None),
            P(),
            P("expert", "dp", None),
            P("expert", None),
            P("expert", ("dp", "seq")),
            P("expert", None),
        ),
        out_specs=(P(), P(("dp", "expert"), "seq", None), P(("dp", "seq", "expert"), None)),
        check_vma=False,
    )
```

profile of v0, /device:TPU:0, one launch (start us, length us, event | category | flops | bytes accessed | tf_op | source)
XLA Modules:
  0.0 226.6 jit_solution(16074221936769703626)
XLA Ops:
  7.2 16.1 %all_gather.9 = bf16[1,8,4096]{2,0,1:T(2,128)(2,1)S(1)} all-gather(bf16[1,1,4096]{2,0,1:T(2,128)(2,1)} %bitcast.151), channel_id=1, replica_groups=mesh['dp'=4,'seq'=2,'expert'=4] {'dp','seq'}, dimensions={1}, use_global_device_ids=true | all-gather | bytes 73728 | tf_op jit(solution)/shard_map/all_gather | solution.py:62
  23.4 0.8 reduce-window.8
  24.3 0.9 select_reduce_fusion.5
  25.8 0.9 fusion.18
  26.7 0.9 fusion.21
  27.7 0.9 fusion.20
  28.6 0.9 fusion.19
  30.4 4.6 %all-to-all-start.1 = ((bf16[1,8,32]{1,0,2:T(2,128)(2,1)}), bf16[1,8,32]{1,0,2:T(2,128)(2,1)S(1)}, u32[]{:S(2)}, u32[]{:S(2)}) async-start(bf16[1,8,32]{1,0,2:T(2,128)(2,1)} %reshape.395), calls=%async_computation.1 | async-start | bytes 32768 | tf_op jit(solution)/shard_map/all_to_all | solution.py:120
  36.0 0.9 reshape_squeeze.6
  38.2 2.4 %all-to-all-done.1 = bf16[1,8,32]{1,0,2:T(2,128)(2,1)S(1)} async-done(((bf16[1,8,32]{1,0,2:T(2,128)(2,1)}), bf16[1,8,32]{1,0,2:T(2,128)(2,1)S(1)}, u32[]{:S(2)}, u32[]{:S(2)}) %all-to-all-start.1) | async-done | bytes 544 | tf_op jit(solution)/shard_map/all_to_all | solution.py:120
  40.6 3.3 %all-to-all-start.2 = ((bf16[1,8,32]{1,0,2:T(2,128)(2,1)}), bf16[1,8,32]{1,0,2:T(2,128)(2,1)S(1)}, u32[]{:S(2)}, u32[]{:S(2)}) async-start(bf16[1,8,32]{1,0,2:T(2,128)(2,1)} %reshape.396), calls=%async_computation.2 | async-start | bytes 32768 | tf_op jit(solution)/shard_map/all_to_all | solution.py:113
  45.3 4.2 %all-to-all-done.2 = bf16[1,8,32]{1,0,2:T(2,128)(2,1)S(1)} async-done(((bf16[1,8,32]{1,0,2:T(2,128)(2,1)}), bf16[1,8,32]{1,0,2:T(2,128)(2,1)S(1)}, u32[]{:S(2)}, u32[]{:S(2)}) %all-to-all-start.2) | async-done | bytes 544 | tf_op jit(solution)/shard_map/all_to_all | solution.py:113
  49.5 3.4 %all-to-all-start = ((bf16[1,8,32,128]{3,1,0,2:T(8,128)(2,1)}), bf16[1,8,32,128]{3,1,0,2:T(8,128)(2,1)S(1)}, u32[]{:S(2)}, u32[]{:S(2)}) async-start(bf16[1,8,32,128]{3,1,0,2:T(8,128)(2,1)} %copy.63), calls=%async_computation | async-start | bytes 131072 | tf_op jit(solution)/shard_map/all_to_all | solution.py:106
  52.9 5.8 %all-to-all-done = bf16[1,8,32,128]{3,1,0,2:T(8,128)(2,1)S(1)} async-done(((bf16[1,8,32,128]{3,1,0,2:T(8,128)(2,1)}), bf16[1,8,32,128]{3,1,0,2:T(8,128)(2,1)S(1)}, u32[]{:S(2)}, u32[]{:S(2)}) %all-to-all-start) | async-done | bytes 65568 | tf_op jit(solution)/shard_map/all_to_all | solution.py:106
  59.3 26.0 %all-reduce = bf16[8,2048]{1,0:T(8,128)(2,1)S(1)} all-reduce(bf16[8,2048]{1,0:T(8,128)(2,1)S(1)} %convolution_convert_fusion.4), channel_id=2, replica_groups=mesh['dp'=4,'seq'=2,'expert'=4] {'dp','seq'}, use_global_device_ids=true, to_apply=%region_7.8.clone | all-reduce | flops 16384 | bytes 65536
  85.3 1.3 multiply_reduce_fusion.3
  87.3 1.8 all-gather
  90.2 11.4 %all_to_all.48 = bf16[16,2,2048]{2,1,0:T(2,128)(2,1)S(1)} all-to-all(bf16[16,2,2048]{2,1,0:T(2,128)(2,1)S(1)} %reshape.371), channel_id=1, replica_groups=mesh['dp'=4,'seq'=2,'expert'=4] {'dp','expert'}, dimensions={0} | all-to-all | bytes 262144 | tf_op jit(solution)/shard_map/all_to_all | solution.py:24
  101.7 1.9 fusion.4
  104.0 1.8 convolution_convert_fusion.2
  106.6 3.5 %all-to-all-start.4 = ((bf16[16,2,2048]{2,1,0:T(2,128)(2,1)}), bf16[16,2,2048]{2,1,0:T(2,128)(2,1)S(1)}, u32[]{:S(2)}, u32[]{:S(2)}) async-start(bf16[16,2,2048]{2,1,0:T(2,128)(2,1)} %copy.70), calls=%async_computation.4 | async-start | bytes 262144 | tf_op jit(solution)/shard_map/all_to_all | solution.py:28
  111.6 6.3 %all-to-all-done.4 = bf16[16,2,2048]{2,1,0:T(2,128)(2,1)S(1)} async-done(((bf16[16,2,2048]{2,1,0:T(2,128)(2,1)}), bf16[16,2,2048]{2,1,0:T(2,128)(2,1)S(1)}, u32[]{:S(2)}, u32[]{:S(2)}) %all-to-all-start.4) | async-done | bytes 131104 | tf_op jit(solution)/shard_map/all_to_all | solution.py:28
  118.1 2.5 %all-reduce.1 = bf16[2,2048]{1,0:T(2,128)(2,1)S(1)} all-reduce(bf16[2,2048]{1,0:T(2,128)(2,1)S(1)} %convolution_convert_fusion.5), channel_id=3, replica_groups=mesh['dp'=4,'seq'=2,'expert'=4] {'seq'}, use_global_device_ids=true, to_apply=%region_16.17.clone | all-reduce | flops 4096 | bytes 16384
  120.6 1.3 multiply_reduce_fusion.2
  125.3 1.8 all-gather.1
  127.9 2.4 %psum.15 = f32[2,8]{1,0:T(2,128)S(1)} all-reduce(f32[2,8]{1,0:T(2,128)S(1)} %select_reduce_fusion.1), channel_id=1, replica_groups=mesh['dp'=4,'seq'=2,'expert'=4] {'seq'}, use_global_device_ids=true, to_apply=%region_23.24 | all-reduce | flops 16 | bytes 128 | tf_op jit(solution)/shard_map/psum | solution.py:210
  131.5 3.5 %all-to-all-start.5 = ((bf16[16,2,2048]{2,1,0:T(2,128)(2,1)}), bf16[16,2,2048]{2,1,0:T(2,128)(2,1)S(1)}, u32[]{:S(2)}, u32[]{:S(2)}) async-start(bf16[16,2,2048]{2,1,0:T(2,128)(2,1)} %reshape.375), calls=%async_computation.5 | async-start | bytes 262144 | tf_op jit(solution)/shard_map/all_to_all | solution.py:24
  135.0 1.2 fusion.64
  140.3 41.4 %psum.14 = f32[]{:T(128)} all-reduce(f32[]{:T(128)} %bitcast.38), channel_id=1, replica_groups=mesh['dp'=4,'seq'=2,'expert'=4] {'dp','seq','expert'}, use_global_device_ids=true, to_apply=%region_19.20 | all-reduce | flops 1 | bytes 8 | tf_op jit(solution)/shard_map/psum | solution.py:190
  181.7 34.8 %reduce-scatter.4.cloned.1.call-done = f32[64,16]{1,0:T(8,128)} async-done(((f32[1024,16]{1,0:T(8,128)}), f32[64,16]{1,0:T(8,128)}) %reduce-scatter.4.cloned.1.call-update) | async-done | bytes 4112
  216.5 1.4 copy.77
  218.0 1.7 fusion
  (87 shorter events, 12.6 us)
Async XLA Ops:
  7.2 51.7 %copy-start = (bf16[512,2048]{1,0:T(8,128)(2,1)S(1)}, bf16[512,2048]{1,0:T(8,128)(2,1)}, u32[]{:S(2)}) copy-start(bf16[512,2048]{1,0:T(8,128)(2,1)} %param.19) | copy-start | bytes 6291460
  7.2 37.5 %copy-start.8 = (u32[32]{0:T(128)S(1)}, u32[32]{0:T(128)}, u32[]{:S(2)}) copy-start(u32[32]{0:T(128)} %constant.81) | copy-start | bytes 388
  7.2 36.8 %copy-start.3 = (s32[1,2,8]{2,1,0:T(2,128)S(1)}, s32[1,2,8]{2,1,0:T(2,128)}, u32[]{:S(2)}) copy-start(s32[1,2,8]{2,1,0:T(2,128)} %param.26) | copy-start | bytes 196
  7.2 36.8 %copy-start.5 = (bf16[2048]{0:T(1024)(128)(2,1)S(1)}, bf16[2048]{0:T(1024)(128)(2,1)}, u32[]{:S(2)}) copy-start(bf16[2048]{0:T(1024)(128)(2,1)} %param.20) | copy-start | bytes 12292
  30.4 10.3 %all-to-all-start.1 = ((bf16[1,8,32]{1,0,2:T(2,128)(2,1)}), bf16[1,8,32]{1,0,2:T(2,128)(2,1)S(1)}, u32[]{:S(2)}, u32[]{:S(2)}) async-start(bf16[1,8,32]{1,0,2:T(2,128)(2,1)} %reshape.395), calls=%async_computation.1 | async-start | bytes 32768 | tf_op jit(solution)/shard_map/all_to_all | solution.py:120
  37.2 48.1 %copy-start.4 = (bf16[1,1,2048]{2,1,0:T(2,128)(2,1)S(1)}, bf16[1,1,2048]{2,1,0:T(2,128)(2,1)}, u32[]{:S(2)}) copy-start(bf16[1,1,2048]{2,1,0:T(2,128)(2,1)} %param.18) | copy-start | bytes 12292
  37.2 51.9 %copy-start.6 = (bf16[2048,16]{0,1:T(8,128)(2,1)S(1)}, bf16[2048,16]{0,1:T(8,128)(2,1)}, u32[]{:S(2)}) copy-start(bf16[2048,16]{0,1:T(8,128)(2,1)} %param.21) | copy-start | bytes 196612
  40.6 8.9 %all-to-all-start.2 = ((bf16[1,8,32]{1,0,2:T(2,128)(2,1)}), bf16[1,8,32]{1,0,2:T(2,128)(2,1)S(1)}, u32[]{:S(2)}, u32[]{:S(2)}) async-start(bf16[1,8,32]{1,0,2:T(2,128)(2,1)} %reshape.396), calls=%async_computation.2 | async-start | bytes 32768 | tf_op jit(solution)/shard_map/all_to_all | solution.py:113
  49.5 9.2 %all-to-all-start = ((bf16[1,8,32,128]{3,1,0,2:T(8,128)(2,1)}), bf16[1,8,32,128]{3,1,0,2:T(8,128)(2,1)S(1)}, u32[]{:S(2)}, u32[]{:S(2)}) async-start(bf16[1,8,32,128]{3,1,0,2:T(8,128)(2,1)} %copy.63), calls=%async_computation | async-start | bytes 131072 | tf_op jit(solution)/shard_map/all_to_all | solution.py:106
  101.7 1.9 copy-start.1
  103.9 6.8 %copy-start.7 = (u32[32]{0:T(128)S(1)}, u32[32]{0:T(128)}, u32[]{:S(2)}) copy-start(u32[32]{0:T(128)} %constant.85) | copy-start | bytes 388
  104.0 7.4 %copy-start.2 = (bf16[2048]{0:T(1024)(128)(2,1)S(1)}, bf16[2048]{0:T(1024)(128)(2,1)}, u32[]{:S(2)}) copy-start(bf16[2048]{0:T(1024)(128)(2,1)} %param.25) | copy-start | bytes 12292
  106.6 11.3 %all-to-all-start.4 = ((bf16[16,2,2048]{2,1,0:T(2,128)(2,1)}), bf16[16,2,2048]{2,1,0:T(2,128)(2,1)S(1)}, u32[]{:S(2)}, u32[]{:S(2)}) async-start(bf16[16,2,2048]{2,1,0:T(2,128)(2,1)} %copy.70), calls=%async_computation.4 | async-start | bytes 262144 | tf_op jit(solution)/shard_map/all_to_all | solution.py:28
  131.5 86.5 %all-to-all-start.5 = ((bf16[16,2,2048]{2,1,0:T(2,128)(2,1)}), bf16[16,2,2048]{2,1,0:T(2,128)(2,1)S(1)}, u32[]{:S(2)}, u32[]{:S(2)}) async-start(bf16[16,2,2048]{2,1,0:T(2,128)(2,1)} %reshape.375), calls=%async_computation.5 | async-start | bytes 262144 | tf_op jit(solution)/shard_map/all_to_all | solution.py:24
  135.0 81.5 %reduce-scatter.4.cloned.1.call-start = ((), (), s32[]{:S(2)}) async-start(), calls=%async_computation.7 | async-start | bytes 557056
Sparse Core Ops, SparseCore 0:
  138.6 77.8 reduce-scatter.3
where the time goes:
time: 228 us; the launch traced here: 227 us
  blocking collectives  103 us (45%)
  waiting for transfers between devices  53.6 us (24%)
  between operations  21.8 us (10%)
  starting transfers between devices  18.3 us (8%)
  matrix products  12.4 us (5%)
  local copies, waits for them, and re-layouts  8.71 us (4%)
  other arithmetic  8.21 us (4%)
    psum x1, blocking collectives, shards(): loss = lax.psum(local_loss, ('dp', 'seq', 'expert'))  41.4 us
    unnamed x2, waiting for transfers between devices  34.8 us
    unnamed x2, blocking collectives  28.5 us
    all_gather x1, blocking collectives, shards(): query_all = lax.all_gather(queries, ('dp', 'seq'), axis=1, tiled=True)[0]  16.1 us
    all_to_all x1, blocking collectives, move_rows(): lax.all_to_all(buffer, ('dp', 'expert'), split_axis=0, concat_axis=0, til...  11.4 us
    all_to_all x1, waiting for transfers between devices, move_back(): lax.all_to_all(buffer.astype(jnp.bfloat16), ('dp', 'expert'), split_axis=...  6.27 us
    all_to_all x1, waiting for transfers between devices, shards(): lax.all_to_all(weighted.reshape(1, number_of_steps, QUERY_HEADS, HEAD_WID...  5.81 us
    all_to_all x1, starting transfers between devices, shards(): lax.all_to_all(local_peak.reshape(1, number_of_steps, QUERY_HEADS).astype...  4.6 us
  transfers between devices with their start and end apart: 6, of which 5 were waited for; matrix products, arithmetic and copies ran while one was open for 4% of the time, Pallas kernels for 0%

commit v1 on v0

v1 whole, which is shorter than its diff:
```python
import functools

import jax
import jax.numpy as jnp
from jax import lax
from jax.experimental import pallas as pl
from jax.experimental.pallas import tpu as pltpu
from jax.sharding import PartitionSpec as P

QUERY_HEADS = 32
KEY_VALUE_HEADS = 4
HEAD_WIDTH = 128
LANES = 128
MASKED = -1e30
EPSILON = 1e-06
MESH = pl.DeviceIdType.MESH
F32 = jnp.float32
BF16 = jnp.bfloat16


def iota(shape, axis):
    return lax.broadcasted_iota(jnp.int32, shape, axis)


def total(x):
    return jnp.sum(jnp.sum(x, axis=1, keepdims=True), axis=0, keepdims=True)


def to_row(column, n):
    eye = iota((n, n), 0) == iota((n, n), 1)
    return jnp.sum(jnp.where(eye, column, 0.0), axis=0, keepdims=True)


def to_column(row, n):
    eye = iota((n, n), 0) == iota((n, n), 1)
    return jnp.sum(jnp.where(eye, row, 0.0), axis=1, keepdims=True)


def kernel(
    sizes,
    keys,
    values,
    queries,
    residual,
    out_proj,
    gain,
    router,
    w_gate,
    w_up,
    w_down,
    head,
    routes,
    step_pos,
    labels,
    trace_len,
    loss_out,
    hidden_out,
    grads_out,
    router_out,
    key_v,
    value_v,
    proj_v,
    gate_v,
    up_v,
    down_v,
    q_own,
    q_buf,
    q_f32,
    part_send,
    part_buf,
    stat_send,
    stat_buf,
    mix_f32,
    mix_send,
    mix_buf,
    norm_own,
    norm_buf,
    norm_f32,
    rows,
    out_f32,
    out_send,
    out_buf,
    grad_send,
    grad_buf,
    grad_f32,
    dlog_own,
    dlog_buf,
    load_sem,
    send_sem,
    recv_sem,
):
    DP, SQ, EN = sizes
    G, E = DP * SQ, DP * EN
    N = G * EN
    width = residual.shape[1]
    WB = width // LANES
    dp, sq, ex = lax.axis_index("dp"), lax.axis_index("seq"), lax.axis_index("expert")
    mine = dp * SQ + sq
    me = ex * G + mine
    tokens = keys.shape[1]

    loads = [
        pltpu.make_async_copy(source.at[0] if cut else source, target, load_sem.at[i])
        for i, (source, target, cut) in enumerate(
            [
                (keys, key_v, True),
                (values, value_v, True),
                (out_proj, proj_v, False),
                (w_gate, gate_v, True),
                (w_up, up_v, True),
                (w_down, down_v, True),
            ]
        )
    ]
    for load in loads:
        load.start()

    def device(t):
        place = lax.rem(t, G)
        return (place // SQ, lax.rem(place, SQ), t // G)

    barrier = pltpu.get_barrier_semaphore()

    def greet(i, carry):
        pl.semaphore_signal(
            barrier, inc=1, device_id=device(lax.rem(me + i, N)), device_id_type=MESH
        )
        return carry

    lax.fori_loop(1, N, greet, 0)

    def send(source, target, number, to):
        pltpu.make_async_remote_copy(
            src_ref=source,
            dst_ref=target,
            send_sem=send_sem.at[number],
            recv_sem=recv_sem.at[number],
            device_id=to,
            device_id_type=MESH,
        ).start()

    def to_pack(body):
        def step(i, carry):
            place = lax.rem(mine + i, G)
            body(place, (place // SQ, lax.rem(place, SQ), ex))
            return carry

        lax.fori_loop(1, G, step, 0)

    def to_all(body):
        def step(i, carry):
            t = lax.rem(me + i, N)
            body(t, device(t))
            return carry

        lax.fori_loop(1, N, step, 0)

    def await_all(buf, count, sem):
        span = buf.at[pl.ds(0, count)]
        pltpu.make_async_copy(span, span, sem).wait()

    q_row = queries[...].astype(F32)
    q_own[...] = jnp.concatenate(
        [q_row[:, h * LANES : (h + 1) * LANES] for h in range(QUERY_HEADS)], axis=0
    ).astype(BF16)

    traces = trace_len.shape[1]
    pos_col = to_column(step_pos[...].astype(F32), G)
    len_row = trace_len[...].astype(F32)
    len_col = to_column(len_row, traces)
    before = iota((traces, traces), 0) <= iota((traces, traces), 1)
    ends_row = jnp.sum(jnp.where(before, len_col, 0.0), axis=0, keepdims=True)
    start_col = jnp.sum(jnp.where(ends_row <= pos_col, len_row, 0.0), axis=1, keepdims=True)
    key_pos = (mine * tokens + iota((G, tokens), 1)).astype(F32)
    allowed = jnp.where((key_pos <= pos_col) & (key_pos >= start_col), 1.0, 0.0)
    group = QUERY_HEADS // KEY_VALUE_HEADS
    allowed = jnp.concatenate([allowed] * group, axis=0) > 0.5

    pl.semaphore_wait(barrier, N - 1)

    to_pack(lambda place, to: send(q_own, q_buf.at[mine], 0, to))
    q_buf[mine] = q_own[...]
    loads[0].wait()
    loads[1].wait()
    await_all(q_buf, G - 1, recv_sem.at[0])

    q_f32[...] = q_buf[...].astype(F32).reshape(G * QUERY_HEADS, LANES)
    peaks, sums = [], []
    per_group = KEY_VALUE_HEADS
    owners = G // per_group
    for g in range(KEY_VALUE_HEADS):
        q_part = jnp.concatenate(
            [q_f32[pl.ds(g * group + h, G, stride=QUERY_HEADS), :] for h in range(group)], axis=0
        ).astype(BF16)
        columns = slice(g * HEAD_WIDTH, (g + 1) * HEAD_WIDTH)
        score = (
            lax.dot_general(
                q_part, key_v[:, columns], (((1,), (1,)), ((), ())), preferred_element_type=F32
            )
            * HEAD_WIDTH ** (-0.5)
        )
        score = jnp.where(allowed, score, MASKED)
        peak = jnp.max(score, axis=1, keepdims=True)
        weight = jnp.where(allowed, jnp.exp(score - peak), 0.0)
        peaks.append(peak)
        sums.append(jnp.sum(weight, axis=1, keepdims=True))
        part = jnp.dot(weight.astype(BF16), value_v[:, columns], preferred_element_type=F32)
        part_send[g * owners : (g + 1) * owners] = part.astype(BF16).reshape(
            owners, QUERY_HEADS, LANES
        )
    peaks, sums = jnp.concatenate(peaks, axis=0), jnp.concatenate(sums, axis=0)
    for b in range(G * QUERY_HEADS // LANES):
        span = slice(b * LANES, (b + 1) * LANES)
        stat_send[b] = jnp.concatenate(
            [to_row(peaks[span], LANES), to_row(sums[span], LANES), jnp.zeros((6, LANES), F32)],
            axis=0,
        )
    per_block = LANES // QUERY_HEADS

    def send_parts(place, to):
        send(stat_send.at[place // per_block], stat_buf.at[mine], 2, to)
        send(part_send.at[place], part_buf.at[mine], 1, to)

    to_pack(send_parts)
    part_buf[mine] = part_send[mine]
    stat_buf[mine] = stat_send[mine // per_block]
    loads[2].wait()
    await_all(stat_buf, G - 1, recv_sem.at[2])
    await_all(part_buf, G - 1, recv_sem.at[1])

    lane = iota((QUERY_HEADS, LANES), 1)
    pick = lane == lax.rem(mine, per_block) * QUERY_HEADS + iota((QUERY_HEADS, LANES), 0)
    peak_of, sum_of = [], []
    for s in range(G):
        stat = stat_buf[s]
        peak_of.append(jnp.sum(jnp.where(pick, stat[0:1], 0.0), axis=1, keepdims=True))
        sum_of.append(jnp.sum(jnp.where(pick, stat[1:2], 0.0), axis=1, keepdims=True))
    peak_all = functools.reduce(jnp.maximum, peak_of)
    weighted = jnp.zeros((QUERY_HEADS, LANES), F32)
    sum_all = jnp.zeros((QUERY_HEADS, 1), F32)
    for s in range(G):
        factor = jnp.exp(peak_of[s] - peak_all)
        weighted += part_buf[s].astype(F32) * factor
        sum_all += sum_of[s] * factor
    attn = weighted / sum_all
    attn = jnp.concatenate(
        [attn[h * G : (h + 1) * G] for h in range(QUERY_HEADS // G)], axis=1
    ).astype(BF16)
    mixed = jnp.dot(attn, proj_v[...], preferred_element_type=F32)
    for c in range(WB):
        mix_f32[pl.ds(c, G, stride=WB), :] = mixed[:, c * LANES : (c + 1) * LANES]
    mix_send[...] = mix_f32[...].astype(BF16).reshape(G, WB, LANES)

    to_pack(lambda place, to: send(mix_send.at[place], mix_buf.at[mine], 3, to))
    mix_buf[mine] = mix_send[mine]
    res_row = residual[...].astype(F32)
    stream = jnp.concatenate(
        [res_row[:, c * LANES : (c + 1) * LANES] for c in range(WB)], axis=0
    )
    head_f32 = head[...].astype(F32)
    await_all(mix_buf, G - 1, recv_sem.at[3])
    stream += jnp.sum(mix_buf[...].astype(F32), axis=0)
    scale = lax.rsqrt(total(stream * stream) * (1.0 / width) + EPSILON)
    normed = (stream * scale * gain[...].astype(F32)).astype(BF16)
    norm_own[...] = normed

    to_all(lambda t, to: send(norm_own, norm_buf.at[me], 4, to))
    norm_buf[me] = norm_own[...]

    normed = normed.astype(F32)
    logits = jnp.zeros((E, LANES), F32)
    for c in range(WB):
        logits += router[:, c * LANES : (c + 1) * LANES].astype(F32) * normed[c : c + 1]
    logits = jnp.sum(logits, axis=1, keepdims=True)
    route_row = routes[pl.ds(sq, 1), :].astype(F32)
    topk = routes.shape[1]
    chosen = jnp.sum(
        jnp.where(iota((E, topk), 0).astype(F32) == route_row, 1.0, 0.0), axis=1, keepdims=True
    )
    masked = jnp.where(chosen > 0.5, logits, MASKED)
    power = jnp.where(
        chosen > 0.5, jnp.exp(masked - jnp.max(masked, axis=0, keepdims=True)), 0.0
    )
    gate_weight = power / jnp.sum(power, axis=0, keepdims=True)

    for load in loads[3:]:
        load.wait()
    await_all(norm_buf, N - 1, recv_sem.at[4])

    norm_f32[...] = norm_buf[...].astype(F32).reshape(N * WB, LANES)
    for c in range(WB):
        rows[:, c * LANES : (c + 1) * LANES] = norm_f32[pl.ds(c, N, stride=WB), :].astype(BF16)
    gate_act = jnp.dot(rows[...], gate_v[...], preferred_element_type=F32)
    up_act = jnp.dot(rows[...], up_v[...], preferred_element_type=F32)
    hidden = (gate_act / (1.0 + jnp.exp(-gate_act)) * up_act).astype(BF16)
    hidden_out[...] = hidden
    expert_out = jnp.dot(hidden, down_v[...], preferred_element_type=F32)
    for c in range(WB):
        out_f32[pl.ds(c, N, stride=WB), :] = expert_out[:, c * LANES : (c + 1) * LANES]
    out_send[...] = out_f32[...].astype(BF16).reshape(N, WB, LANES)

    slot = sq * E + dp * EN + ex
    to_all(lambda t, to: send(out_send.at[t], out_buf.at[slot], 5, to))
    out_buf[slot] = out_send[me]
    await_all(out_buf, N - 1, recv_sem.at[5])

    outs = out_buf[0:E].astype(F32)
    for half in range(1, SQ):
        outs += out_buf[half * E : (half + 1) * E].astype(F32)
    final = stream + jnp.sum(outs * gate_weight.reshape(E, 1, 1), axis=0)
    scale = lax.rsqrt(total(final * final) * (1.0 / width) + EPSILON)
    along = total(final * head_f32)
    reward = along * scale
    target = labels[...].astype(F32)
    decay = jnp.exp(-jnp.abs(reward))
    row_loss = jnp.maximum(reward, 0.0) + jnp.log1p(decay) - target * reward
    error = jnp.where(reward >= 0.0, 1.0, decay) / (1.0 + decay) - target
    d_mix = (
        (error * scale) * (head_f32 - final * (scale * scale * along * (1.0 / width)))
    ).astype(BF16).astype(F32)
    grad_send[...] = (gate_weight.reshape(E, 1, 1) * d_mix[None]).astype(BF16)

    to_all(
        lambda t, to: send(
            grad_send.at[to[0] * EN + to[2]], grad_buf.at[me], 6, to
        )
    )
    grad_buf[me] = grad_send[dp * EN + ex]
    route_dot = jnp.sum(jnp.sum(outs * d_mix[None], axis=1), axis=1, keepdims=True)
    mean_dot = jnp.sum(gate_weight * route_dot, axis=0, keepdims=True)
    d_logits = to_row(gate_weight * (route_dot - mean_dot), E)
    if E < LANES:
        d_logits = jnp.concatenate([d_logits, jnp.zeros((1, LANES - E), F32)], axis=1)
    dlog_own[...] = jnp.concatenate(
        [d_logits, jnp.broadcast_to(row_loss, (1, LANES))], axis=0
    )
    to_all(lambda t, to: send(dlog_own, dlog_buf.at[me], 7, to))
    dlog_buf[me] = dlog_own[...]

    await_all(grad_buf, N - 1, recv_sem.at[6])
    grad_f32[...] = grad_buf[...].astype(F32).reshape(N * WB, LANES)
    for c in range(WB):
        grads_out[:, c * LANES : (c + 1) * LANES] = grad_f32[
            pl.ds(c, N, stride=WB), :
        ].astype(BF16)

    share = width // N
    first = ((dp * SQ + sq) * EN + ex) * share
    own_columns = norm_f32[pl.ds(first // LANES, N, stride=WB), :]
    own_columns = pltpu.roll(own_columns, lax.rem(LANES - lax.rem(first, LANES), LANES), 1)
    await_all(dlog_buf, N - 1, recv_sem.at[7])
    loss_out[...] = jnp.sum(dlog_buf[:, 1, :], axis=0, keepdims=True)
    router_grad = lax.dot_general(
        dlog_buf[:, 0, :],
        own_columns,
        (((0,), (0,)), ((), ())),
        precision=lax.Precision.HIGHEST,
        preferred_element_type=F32,
    )
    router_out[...] = router_grad[0:E, 0:share].astype(BF16)

    for number, (buf, count) in enumerate(
        [
            (q_buf, G),
            (part_buf, G),
            (stat_buf, G),
            (mix_buf, G),
            (norm_buf, N),
            (out_buf, N),
            (grad_buf, N),
            (dlog_buf, N),
        ]
    ):
        await_all(buf, count - 1, send_sem.at[number])


def shards(
    sizes,
    keys,
    values,
    queries,
    residual,
    out_proj,
    norm_gain,
    router,
    w_gate,
    w_up,
    w_down,
    head_vec,
    routes,
    step_pos,
    labels,
    trace_len,
):
    DP, SQ, EN = sizes
    G, E = DP * SQ, DP * EN
    N = G * EN
    width = residual.shape[2]
    WB = width // LANES
    hidden_units = w_gate.shape[2]
    hbm = pl.BlockSpec(memory_space=pl.ANY)
    vmem = pl.BlockSpec(memory_space=pltpu.VMEM)
    message = (WB, LANES)
    loss, hidden, grads, grad_router = pl.pallas_call(
        functools.partial(kernel, sizes),
        out_shape=(
            jax.ShapeDtypeStruct((1, LANES), F32),
            jax.ShapeDtypeStruct((N, hidden_units), BF16),
            jax.ShapeDtypeStruct((N, width), BF16),
            jax.ShapeDtypeStruct((E, width // N), BF16),
        ),
        in_specs=[hbm, hbm, vmem, vmem, hbm, vmem, vmem, hbm, hbm, hbm, vmem, vmem, vmem, vmem, vmem],
        out_specs=(vmem, vmem, vmem, vmem),
        scratch_shapes=[
            pltpu.VMEM(keys.shape[1:], BF16),
            pltpu.VMEM(values.shape[1:], BF16),
            pltpu.VMEM(out_proj.shape, BF16),
            pltpu.VMEM(w_gate.shape[1:], BF16),
            pltpu.VMEM(w_up.shape[1:], BF16),
            pltpu.VMEM(w_down.shape[1:], BF16),
            pltpu.VMEM((QUERY_HEADS, LANES), BF16),
            pltpu.VMEM((G, QUERY_HEADS, LANES), BF16),
            pltpu.VMEM((G * QUERY_HEADS, LANES), F32),
            pltpu.VMEM((G, QUERY_HEADS, LANES), BF16),
            pltpu.VMEM((G, QUERY_HEADS, LANES), BF16),
            pltpu.VMEM((G * QUERY_HEADS // LANES, 8, LANES), F32),
            pltpu.VMEM((G, 8, LANES), F32),
            pltpu.VMEM((G * WB, LANES), F32),
            pltpu.VMEM((G,) + message, BF16),
            pltpu.VMEM((G,) + message, BF16),
            pltpu.VMEM(message, BF16),
            pltpu.VMEM((N,) + message, BF16),
            pltpu.VMEM((N * WB, LANES), F32),
            pltpu.VMEM((N, width), BF16),
            pltpu.VMEM((N * WB, LANES), F32),
            pltpu.VMEM((N,) + message, BF16),
            pltpu.VMEM((N,) + message, BF16),
            pltpu.VMEM((E,) + message, BF16),
            pltpu.VMEM((N,) + message, BF16),
            pltpu.VMEM((N * WB, LANES), F32),
            pltpu.VMEM((2, LANES), F32),
            pltpu.VMEM((N, 2, LANES), F32),
            pltpu.SemaphoreType.DMA((6,)),
            pltpu.SemaphoreType.DMA((8,)),
            pltpu.SemaphoreType.DMA((8,)),
        ],
        compiler_params=pltpu.CompilerParams(
            collective_id=0, has_side_effects=True, vmem_limit_bytes=56 * 1024 * 1024
        ),
    )(
        keys,
        values,
        queries[0],
        residual[0],
        out_proj,
        norm_gain.reshape(message),
        router.T,
        w_gate,
        w_up,
        w_down,
        head_vec.reshape(message),
        routes[0],
        step_pos,
        labels,
        trace_len,
    )
    grad_down = lax.dot_general(
        hidden, grads, (((0,), (0,)), ((), ())), preferred_element_type=F32
    ).astype(BF16)
    return loss[0, 0], grad_down[None], grad_router.T


def solution(mesh):
    sizes = (mesh.shape["dp"], mesh.shape["seq"], mesh.shape["expert"])
    return jax.shard_map(
        functools.partial(shards, sizes),
        mesh=mesh,
        in_specs=(
            P("expert", ("dp", "seq"), None),
            P("expert", ("dp", "seq"), None),
            P("expert", ("dp", "seq"), None),
            P("expert", ("dp", "seq"), None),
            P(("dp", "seq"), None),
            P(),
            P(),
            P(("dp", "expert"), None, "seq"),
            P(("dp", "expert"), None, "seq"),
            P(("dp", "expert"), "seq", None),
            P(),
            P("expert", "dp", None),
            P("expert", None),
            P("expert", ("dp", "seq")),
            P("expert", None),
        ),
        out_specs=(P(), P(("dp", "expert"), "seq", None), P(("dp", "seq", "expert"), None)),
        check_vma=False,
    )
```

time: 228 us -> 45.8 us (0.20)
  the two profiles are of different devices: /device:TPU:0 before, /device:TPU:1 now
where the time goes in v1:
time: 45.8 us; the launch traced here: 45.2 us
  Pallas kernels  39.5 us (86%)
  matrix products  2.66 us (6%)
  between operations  2.49 us (5%)
  local copies, waits for them, and re-layouts  0.6 us (1%)
    pallas_call x1, Pallas kernels, shards(): pl.pallas_call(functools.partial(kernel, sizes), out_shape=(jax.ShapeDtyp...  39.5 us
    dot_general x1, matrix products, shards(): lax.dot_general(hidden, grads, (((0,), (0,)), ((), ())), preferred_elemen...  2.66 us

profile of v1, /device:TPU:1, one launch (start us, length us, event | category | flops | bytes accessed | tf_op | source)
XLA Modules:
  0.0 45.2 jit_solution(550247547738364878)
XLA Ops:
  1.3 39.5 %shard_map.166 = (f32[1,128]{1,0:T(1,128)}, bf16[32,384]{1,0:T(8,128)(2,1)}, bf16[32,2048]{1,0:T(8,128)(2,1)}, bf16[16,64]{1,0:T(8,128)(2,1)}) custom-call(bf16[1,128,512]{2,1,0:T(8,128)(2,1)} %keys.1, bf16[1,128,512]{2,1,0:T(8,128)(2,1)} %values.1, bf16[1,4096]{1,0:T(2,128)(2,1)} %bitcast.14, bf16[1,2048]{1,0:T(2,128)(2,1)} %bitcast.15, ...), custom_call_target="tpu_custom_call" | custom-call | tf_op jit(solution)/shard_map/pallas_call | solution.py:404
  40.8 0.0 copy-start.1
  40.8 0.0 copy-start
  40.8 2.7 %fusion = bf16[1,384,2048]{2,1,0:T(8,128)(2,1)} fusion(bf16[32,384]{1,0:T(8,128)(2,1)} %get-tuple-element.8, bf16[32,2048]{1,0:T(8,128)(2,1)} %get-tuple-element.9), kind=kOutput, calls=%fused_computation.1 | convolution fusion | flops 51118080 | bytes 1728512 | tf_op jit(solution)/shard_map/dot_general | solution.py:467
  43.5 0.0 copy-done.1
  43.5 0.0 copy-done
  43.5 0.6 %copy.22 = bf16[64,16]{0,1:T(8,128)(2,1)} copy(bf16[64,16]{0,1:T(8,128)(2,1)S(1)} %bitcast.18) | data formatting | bytes 4096
Async XLA Ops:
  40.8 2.7 %copy-start.1 = (f32[1,128]{1,0:T(1,128)S(1)}, f32[1,128]{1,0:T(1,128)}, u32[]{:S(2)}) copy-start(f32[1,128]{1,0:T(1,128)} %get-tuple-element.7) | copy-start | bytes 1540
  40.8 2.7 %copy-start = (bf16[16,64]{1,0:T(8,128)(2,1)S(1)}, bf16[16,64]{1,0:T(8,128)(2,1)}, u32[]{:S(2)}) copy-start(bf16[16,64]{1,0:T(8,128)(2,1)} %get-tuple-element.10) | copy-start | bytes 6148

commit v2 on v1

v2 whole, which is shorter than its diff:
```python
import functools

import jax
import jax.numpy as jnp
from jax import lax
from jax.experimental import pallas as pl
from jax.experimental.pallas import tpu as pltpu
from jax.sharding import PartitionSpec as P

QUERY_HEADS = 32
KEY_VALUE_HEADS = 4
HEAD_WIDTH = 128
LANES = 128
MASKED = -1e30
EPSILON = 1e-06
STAT_ROWS = 16
INPUTS = (
    "queries",
    "step_pos",
    "trace_len",
    "keys",
    "values",
    "residual",
    "norm_gain",
    "router",
    "head_vec",
    "routes",
    "labels",
    "out_proj",
    "w_gate",
    "w_up",
    "w_down",
)
MESH = pl.DeviceIdType.MESH
F32 = jnp.float32
BF16 = jnp.bfloat16


def iota(shape, axis):
    return lax.broadcasted_iota(jnp.int32, shape, axis)


def total(x):
    return jnp.sum(jnp.sum(x, axis=1, keepdims=True), axis=0, keepdims=True)


def to_row(column, n):
    eye = iota((n, n), 0) == iota((n, n), 1)
    return jnp.sum(jnp.where(eye, column, 0.0), axis=0, keepdims=True)


def to_column(row, n):
    eye = iota((n, n), 0) == iota((n, n), 1)
    return jnp.sum(jnp.where(eye, row, 0.0), axis=1, keepdims=True)


def split3(x):
    high = x.astype(BF16).astype(F32)
    rest = x - high
    middle = rest.astype(BF16).astype(F32)
    return [high, middle, rest - middle]


def kernel(sizes, names, *refs):
    r = dict(zip(names, refs))
    DP, SQ, EN = sizes
    G, E = DP * SQ, DP * EN
    N = G * EN
    unroll = N <= 32
    proj_v, gate_v, up_v, down_v = r["out_proj"], r["w_gate"], r["w_up"], r["w_down"]
    width = proj_v.shape[1]
    WB = width // LANES
    dp, sq, ex = lax.axis_index("dp"), lax.axis_index("seq"), lax.axis_index("expert")
    mine = dp * SQ + sq
    expert = dp * EN + ex
    me = sq * E + expert
    tokens = r["keys"].shape[0]
    load_sem, send_sem, recv_sem = r["load_sem"], r["send_sem"], r["recv_sem"]

    loads = {}
    for i, name in enumerate(INPUTS):
        source, target = r["in_" + name], r[name]
        if len(source.shape) > len(target.shape):
            source = source.at[0]
        loads[name] = pltpu.make_async_copy(source, target, load_sem.at[i])
        loads[name].start()

    if unroll:
        near_dp = [lax.rem(dp + a, DP) for a in range(DP)]
        near_sq = [lax.rem(sq + a, SQ) for a in range(SQ)]
        near_ex = [lax.rem(ex + a, EN) for a in range(EN)]

        def near(a, b, c):
            return near_dp[a], near_sq[b], near_ex[c]
    else:

        def near(a, b, c):
            return lax.rem(dp + a, DP), lax.rem(sq + b, SQ), lax.rem(ex + c, EN)

    def each(first, last, body):
        if unroll:
            for i in range(first, last):
                body(i)
        else:

            def step(i, carry):
                body(i)
                return carry

            lax.fori_loop(first, last, step, 0)

    def to_pack(body):
        each(1, G, lambda i: body(near(i // SQ, i % SQ, 0)))

    def to_plane(body):
        each(1, E, lambda i: body(near(i // EN, 0, i % EN)))

    def to_pair(body):
        each(1, SQ, lambda i: body(near(0, i, 0)))

    barrier = pltpu.get_barrier_semaphore()

    def greet(to):
        pl.semaphore_signal(barrier, inc=1, device_id=to, device_id_type=MESH)

    to_pack(greet)
    each(1, EN, lambda c: each(0, DP, lambda a: greet(near(a, 0, c))))
    partners = G - 1 + (EN - 1) * DP

    def send(source, target, number, to):
        pltpu.make_async_remote_copy(
            src_ref=source,
            dst_ref=target,
            send_sem=send_sem.at[number],
            recv_sem=recv_sem.at[number],
            device_id=to,
            device_id_type=MESH,
        ).start()

    def await_all(buf, count, sem):
        span = buf.at[pl.ds(0, count)]
        pltpu.make_async_copy(span, span, sem).wait()

    q_own, q_buf, q_f32 = r["q_own"], r["q_buf"], r["q_f32"]
    loads["queries"].wait()
    q_row = r["queries"][...].astype(F32)
    q_own[...] = jnp.concatenate(
        [q_row[:, h * LANES : (h + 1) * LANES] for h in range(QUERY_HEADS)], axis=0
    ).astype(BF16)
    pl.semaphore_wait(barrier, partners)

    to_pack(lambda to: send(q_own, q_buf.at[mine], 0, to))
    q_buf[mine] = q_own[...]

    for name in INPUTS:
        if name not in ("queries", "out_proj", "w_gate", "w_up", "w_down"):
            loads[name].wait()
    traces = r["trace_len"].shape[1]
    pos_col = to_column(r["step_pos"][...].astype(F32), G)
    len_row = r["trace_len"][...].astype(F32)
    len_col = to_column(len_row, traces)
    before = iota((traces, traces), 0) <= iota((traces, traces), 1)
    ends_row = jnp.sum(jnp.where(before, len_col, 0.0), axis=0, keepdims=True)
    start_col = jnp.sum(jnp.where(ends_row <= pos_col, len_row, 0.0), axis=1, keepdims=True)
    key_pos = (mine * tokens + iota((G, tokens), 1)).astype(F32)
    allowed = jnp.where((key_pos <= pos_col) & (key_pos >= start_col), 1.0, 0.0)
    group = QUERY_HEADS // KEY_VALUE_HEADS
    allowed = jnp.concatenate([allowed] * group, axis=0) > 0.5
    await_all(q_buf, G - 1, recv_sem.at[0])

    part_send, part_buf = r["part_send"], r["part_buf"]
    key_v, value_v = r["keys"], r["values"]
    q_f32[...] = q_buf[...].astype(F32).reshape(G * QUERY_HEADS, LANES)
    peaks, sums = [], []
    owners = G // KEY_VALUE_HEADS
    for g in range(KEY_VALUE_HEADS):
        q_part = jnp.concatenate(
            [q_f32[pl.ds(g * group + h, G, stride=QUERY_HEADS), :] for h in range(group)], axis=0
        ).astype(BF16)
        columns = slice(g * HEAD_WIDTH, (g + 1) * HEAD_WIDTH)
        score = (
            lax.dot_general(
                q_part, key_v[:, columns], (((1,), (1,)), ((), ())), preferred_element_type=F32
            )
            * HEAD_WIDTH ** (-0.5)
        )
        score = jnp.where(allowed, score, MASKED)
        peak = jnp.max(score, axis=1, keepdims=True)
        weight = jnp.where(allowed, jnp.exp(score - peak), 0.0)
        peaks.append(peak)
        sums.append(jnp.sum(weight, axis=1, keepdims=True))
        part = jnp.dot(weight.astype(BF16), value_v[:, columns], preferred_element_type=F32)
        part_send[g * owners : (g + 1) * owners, 0:QUERY_HEADS] = part.astype(BF16).reshape(
            owners, QUERY_HEADS, LANES
        )
    peaks, sums = jnp.concatenate(peaks, axis=0), jnp.concatenate(sums, axis=0)
    per_block = LANES // QUERY_HEADS
    for b in range(G // per_block):
        span = slice(b * LANES, (b + 1) * LANES)
        stat = jnp.concatenate(
            split3(to_row(peaks[span], LANES))
            + split3(to_row(sums[span], LANES))
            + [jnp.zeros((STAT_ROWS - 6, LANES), F32)],
            axis=0,
        ).astype(BF16)
        part_send[b * per_block : (b + 1) * per_block, QUERY_HEADS:] = jnp.broadcast_to(
            stat[None], (per_block, STAT_ROWS, LANES)
        )

    to_pack(lambda to: send(part_send.at[to[0] * SQ + to[1]], part_buf.at[mine], 1, to))
    part_buf[mine] = part_send[mine]
    loads["out_proj"].wait()
    lane = iota((QUERY_HEADS, LANES), 1)
    pick = lane == lax.rem(mine, per_block) * QUERY_HEADS + iota((QUERY_HEADS, LANES), 0)
    await_all(part_buf, G - 1, recv_sem.at[1])

    peak_of, sum_of = [], []
    for s in range(G):
        stat = part_buf[s, QUERY_HEADS:].astype(F32)
        peak_row = stat[0:1] + stat[1:2] + stat[2:3]
        sum_row = stat[3:4] + stat[4:5] + stat[5:6]
        peak_of.append(jnp.sum(jnp.where(pick, peak_row, 0.0), axis=1, keepdims=True))
        sum_of.append(jnp.sum(jnp.where(pick, sum_row, 0.0), axis=1, keepdims=True))
    peak_all = functools.reduce(jnp.maximum, peak_of)
    weighted = jnp.zeros((QUERY_HEADS, LANES), F32)
    sum_all = jnp.zeros((QUERY_HEADS, 1), F32)
    for s in range(G):
        factor = jnp.exp(peak_of[s] - peak_all)
        weighted += part_buf[s, 0:QUERY_HEADS].astype(F32) * factor
        sum_all += sum_of[s] * factor
    attn = weighted / sum_all
    attn = jnp.concatenate(
        [attn[h * G : (h + 1) * G] for h in range(QUERY_HEADS // G)], axis=1
    ).astype(BF16)
    mixed = jnp.dot(attn, proj_v[...], preferred_element_type=F32)
    mix_f32, mix_send, mix_buf = r["mix_f32"], r["mix_send"], r["mix_buf"]
    for c in range(WB):
        mix_f32[pl.ds(c, G, stride=WB), :] = mixed[:, c * LANES : (c + 1) * LANES]
    mix_send[...] = mix_f32[...].astype(BF16).reshape(G, WB, LANES)

    to_pack(lambda to: send(mix_send.at[to[0] * SQ + to[1]], mix_buf.at[mine], 2, to))
    mix_buf[mine] = mix_send[mine]
    res_row = r["residual"][...].astype(F32)
    stream = jnp.concatenate(
        [res_row[:, c * LANES : (c + 1) * LANES] for c in range(WB)], axis=0
    )
    head_f32 = r["head_vec"][...].astype(F32)
    gain = r["norm_gain"][...].astype(F32)
    await_all(mix_buf, G - 1, recv_sem.at[2])
    stream += jnp.sum(mix_buf[...].astype(F32), axis=0)
    scale = lax.rsqrt(total(stream * stream) * (1.0 / width) + EPSILON)
    normed = (stream * scale * gain).astype(BF16)
    norm_own, norm_buf, norm_f32, rows = r["norm_own"], r["norm_buf"], r["norm_f32"], r["rows"]
    norm_own[...] = normed

    to_plane(lambda to: send(norm_own, norm_buf.at[me], 3, to))
    norm_buf[me] = norm_own[...]
    plane = pl.ds(sq * E, E)

    normed = normed.astype(F32)
    logits = jnp.zeros((E, LANES), F32)
    for c in range(WB):
        logits += r["router"][:, c * LANES : (c + 1) * LANES].astype(F32) * normed[c : c + 1]
    logits = jnp.sum(logits, axis=1, keepdims=True)
    route_row = r["routes"][pl.ds(sq, 1), :].astype(F32)
    topk = r["routes"].shape[1]
    chosen = jnp.sum(
        jnp.where(iota((E, topk), 0).astype(F32) == route_row, 1.0, 0.0), axis=1, keepdims=True
    )
    masked = jnp.where(chosen > 0.5, logits, MASKED)
    power = jnp.where(
        chosen > 0.5, jnp.exp(masked - jnp.max(masked, axis=0, keepdims=True)), 0.0
    )
    gate_weight = power / jnp.sum(power, axis=0, keepdims=True)

    await_all(norm_buf, E - 1, recv_sem.at[3])
    to_pair(lambda to: send(norm_buf.at[plane], norm_buf.at[plane], 4, to))
    for name in ("w_gate", "w_up", "w_down"):
        loads[name].wait()
    await_all(norm_buf, N - E, recv_sem.at[4])

    norm_f32[...] = norm_buf[...].astype(F32).reshape(N * WB, LANES)
    for c in range(WB):
        rows[:, c * LANES : (c + 1) * LANES] = norm_f32[pl.ds(c, N, stride=WB), :].astype(BF16)
    gate_act = jnp.dot(rows[...], gate_v[...], preferred_element_type=F32)
    up_act = jnp.dot(rows[...], up_v[...], preferred_element_type=F32)
    hidden = (gate_act / (1.0 + jnp.exp(-gate_act)) * up_act).astype(BF16)
    r["hidden"][...] = hidden
    stores = [pltpu.make_async_copy(r["hidden"], r["out_hidden"], load_sem.at[0])]
    stores[0].start()
    expert_out = jnp.dot(hidden, down_v[...], preferred_element_type=F32)
    out_f32, half_send, half_buf = r["out_f32"], r["half_send"], r["half_buf"]
    out_send, out_buf = r["out_send"], r["out_buf"]
    for c in range(WB):
        out_f32[pl.ds(c, N, stride=WB), :] = expert_out[:, c * LANES : (c + 1) * LANES]
    half_send[...] = out_f32[...].astype(BF16).reshape(SQ, E, WB, LANES)

    to_pair(lambda to: send(half_send.at[to[1]], half_buf.at[sq], 5, to))
    await_all(half_buf, SQ - 1, recv_sem.at[5])
    outs = out_f32[pl.ds(pl.multiple_of(sq * (E * WB), E * WB), E * WB), :].reshape(E, WB, LANES)
    for i in range(1, SQ):
        outs += half_buf[lax.rem(sq + i, SQ)].astype(F32)
    out_send[...] = outs.astype(BF16)
    to_plane(lambda to: send(out_send.at[to[0] * EN + to[2]], out_buf.at[expert], 6, to))
    out_buf[expert] = out_send[expert]
    own_label = r["labels"][...].astype(F32)
    weight_column = gate_weight.reshape(E, 1, 1)
    await_all(out_buf, E - 1, recv_sem.at[6])

    outs = out_buf[...].astype(F32)
    final = stream + jnp.sum(outs * weight_column, axis=0)
    scale = lax.rsqrt(total(final * final) * (1.0 / width) + EPSILON)
    along = total(final * head_f32)
    reward = along * scale
    decay = jnp.exp(-jnp.abs(reward))
    row_loss = jnp.maximum(reward, 0.0) + jnp.log1p(decay) - own_label * reward
    error = jnp.where(reward >= 0.0, 1.0, decay) / (1.0 + decay) - own_label
    d_mix = (
        (error * scale) * (head_f32 - final * (scale * scale * along * (1.0 / width)))
    ).astype(BF16).astype(F32)
    grad_send, grad_buf, grad_f32 = r["grad_send"], r["grad_buf"], r["grad_f32"]
    dlog_own, dlog_buf = r["dlog_own"], r["dlog_buf"]
    grad_send[...] = (weight_column * d_mix[None]).astype(BF16)

    to_plane(lambda to: send(grad_send.at[to[0] * EN + to[2]], grad_buf.at[me], 7, to))
    grad_buf[me] = grad_send[expert]
    route_dot = jnp.sum(jnp.sum(outs * d_mix[None], axis=1), axis=1, keepdims=True)
    mean_dot = jnp.sum(gate_weight * route_dot, axis=0, keepdims=True)
    d_logits = to_row(gate_weight * (route_dot - mean_dot), E)
    if E < LANES:
        d_logits = jnp.concatenate([d_logits, jnp.zeros((1, LANES - E), F32)], axis=1)
    dlog_own[...] = jnp.concatenate(
        [d_logits, jnp.broadcast_to(row_loss, (1, LANES))], axis=0
    )
    to_plane(lambda to: send(dlog_own, dlog_buf.at[me], 9, to))
    dlog_buf[me] = dlog_own[...]
    share = width // N
    first = (mine * EN + ex) * share
    own_columns = norm_f32[pl.ds(first // LANES, N, stride=WB), :]
    own_columns = pltpu.roll(own_columns, lax.rem(LANES - lax.rem(first, LANES), LANES), 1)

    await_all(grad_buf, E - 1, recv_sem.at[7])
    to_pair(lambda to: send(grad_buf.at[plane], grad_buf.at[plane], 8, to))
    await_all(dlog_buf, E - 1, recv_sem.at[9])
    to_pair(lambda to: send(dlog_buf.at[plane], dlog_buf.at[plane], 10, to))
    await_all(grad_buf, N - E, recv_sem.at[8])
    grad_f32[...] = grad_buf[...].astype(F32).reshape(N * WB, LANES)
    for c in range(WB):
        r["grads"][:, c * LANES : (c + 1) * LANES] = grad_f32[
            pl.ds(c, N, stride=WB), :
        ].astype(BF16)
    stores.append(pltpu.make_async_copy(r["grads"], r["out_grads"], load_sem.at[1]))
    stores[-1].start()
    await_all(dlog_buf, N - E, recv_sem.at[10])
    r["loss"][...] = jnp.sum(dlog_buf[:, 1, :], axis=0, keepdims=True)
    router_grad = lax.dot_general(
        dlog_buf[:, 0, :],
        own_columns,
        (((0,), (0,)), ((), ())),
        precision=lax.Precision.HIGHEST,
        preferred_element_type=F32,
    )
    r["router_grad"][...] = router_grad[0:E, 0:share].astype(BF16)
    stores.append(pltpu.make_async_copy(r["loss"], r["out_loss"], load_sem.at[2]))
    stores[-1].start()
    stores.append(pltpu.make_async_copy(r["router_grad"], r["out_router"], load_sem.at[3]))
    stores[-1].start()

    for number, (buf, count) in enumerate(
        [
            (q_buf, G - 1),
            (part_buf, G - 1),
            (mix_buf, G - 1),
            (norm_buf, E - 1),
            (norm_buf, N - E),
            (half_buf, SQ - 1),
            (out_buf, E - 1),
            (grad_buf, E - 1),
            (grad_buf, N - E),
            (dlog_buf, E - 1),
            (dlog_buf, N - E),
        ]
    ):
        await_all(buf, count, send_sem.at[number])
    for store in stores:
        store.wait()


def down_kernel(*refs):
    sources, (loss_out, down_out, router_out), targets = refs[:4], refs[4:7], refs[7:11]
    stage, sem = refs[11:]
    loads = [
        pltpu.make_async_copy(source, target, sem.at[i])
        for i, (source, target) in enumerate(zip(sources, targets))
    ]
    for load in loads:
        load.start()
    for load in loads:
        load.wait()
    hidden, grads, loss, router_grad = targets
    step = stage.shape[1] // 4
    stores = []
    for i in range(4):
        columns = pl.ds(i * step, step)
        stage[:, i * step : (i + 1) * step] = lax.dot_general(
            hidden[...],
            grads[:, i * step : (i + 1) * step],
            (((0,), (0,)), ((), ())),
            preferred_element_type=F32,
        ).astype(BF16)
        stores.append(
            pltpu.make_async_copy(stage.at[:, columns], down_out.at[0, :, columns], sem.at[i])
        )
        stores[-1].start()
    loss_out[...] = loss[:, 0:1]
    router_out[...] = router_grad[...]
    for store in stores:
        store.wait()


def shards(
    sizes,
    keys,
    values,
    queries,
    residual,
    out_proj,
    norm_gain,
    router,
    w_gate,
    w_up,
    w_down,
    head_vec,
    routes,
    step_pos,
    labels,
    trace_len,
):
    DP, SQ, EN = sizes
    G, E = DP * SQ, DP * EN
    N = G * EN
    width = residual.shape[2]
    WB = width // LANES
    hidden_units = w_gate.shape[2]
    hbm = pl.BlockSpec(memory_space=pl.ANY)
    vmem = pl.BlockSpec(memory_space=pltpu.VMEM)
    message = (WB, LANES)
    operands = dict(
        queries=queries[0],
        step_pos=step_pos,
        trace_len=trace_len,
        keys=keys,
        values=values,
        residual=residual[0],
        norm_gain=norm_gain.reshape(message),
        router=router.T,
        head_vec=head_vec.reshape(message),
        routes=routes[0],
        labels=labels,
        out_proj=out_proj,
        w_gate=w_gate,
        w_up=w_up,
        w_down=w_down,
    )
    outs = dict(
        out_loss=jax.ShapeDtypeStruct((1, LANES), F32),
        out_hidden=jax.ShapeDtypeStruct((N, hidden_units), BF16),
        out_grads=jax.ShapeDtypeStruct((N, width), BF16),
        out_router=jax.ShapeDtypeStruct((E, width // N), BF16),
    )
    scratch = {
        name: pltpu.VMEM(operands[name].shape[-2:], operands[name].dtype) for name in INPUTS
    }
    scratch.update(
        loss=pltpu.VMEM((1, LANES), F32),
        hidden=pltpu.VMEM((N, hidden_units), BF16),
        grads=pltpu.VMEM((N, width), BF16),
        router_grad=pltpu.VMEM((E, width // N), BF16),
        q_own=pltpu.VMEM((QUERY_HEADS, LANES), BF16),
        q_buf=pltpu.VMEM((G, QUERY_HEADS, LANES), BF16),
        q_f32=pltpu.VMEM((G * QUERY_HEADS, LANES), F32),
        part_send=pltpu.VMEM((G, QUERY_HEADS + STAT_ROWS, LANES), BF16),
        part_buf=pltpu.VMEM((G, QUERY_HEADS + STAT_ROWS, LANES), BF16),
        mix_f32=pltpu.VMEM((G * WB, LANES), F32),
        mix_send=pltpu.VMEM((G,) + message, BF16),
        mix_buf=pltpu.VMEM((G,) + message, BF16),
        norm_own=pltpu.VMEM(message, BF16),
        norm_buf=pltpu.VMEM((N,) + message, BF16),
        norm_f32=pltpu.VMEM((N * WB, LANES), F32),
        rows=pltpu.VMEM((N, width), BF16),
        out_f32=pltpu.VMEM((N * WB, LANES), F32),
        half_send=pltpu.VMEM((SQ, E) + message, BF16),
        half_buf=pltpu.VMEM((SQ, E) + message, BF16),
        out_send=pltpu.VMEM((E,) + message, BF16),
        out_buf=pltpu.VMEM((E,) + message, BF16),
        grad_send=pltpu.VMEM((E,) + message, BF16),
        grad_buf=pltpu.VMEM((N,) + message, BF16),
        grad_f32=pltpu.VMEM((N * WB, LANES), F32),
        dlog_own=pltpu.VMEM((2, LANES), F32),
        dlog_buf=pltpu.VMEM((N, 2, LANES), F32),
        load_sem=pltpu.SemaphoreType.DMA((len(INPUTS),)),
        send_sem=pltpu.SemaphoreType.DMA((11,)),
        recv_sem=pltpu.SemaphoreType.DMA((11,)),
    )
    names = ["in_" + name for name in INPUTS] + list(outs) + list(scratch)
    loss, hidden, grads, grad_router = pl.pallas_call(
        functools.partial(kernel, sizes, names),
        out_shape=tuple(outs.values()),
        in_specs=[hbm] * len(INPUTS),
        out_specs=(hbm,) * len(outs),
        scratch_shapes=list(scratch.values()),
        compiler_params=pltpu.CompilerParams(
            collective_id=0, has_side_effects=True, vmem_limit_bytes=56 * 1024 * 1024
        ),
    )(*[operands[name] for name in INPUTS])
    loss, grad_down, grad_router = pl.pallas_call(
        down_kernel,
        out_shape=(
            jax.ShapeDtypeStruct((1, 1), F32),
            jax.ShapeDtypeStruct((1, hidden_units, width), BF16),
            jax.ShapeDtypeStruct((E, width // N), BF16),
        ),
        in_specs=[hbm] * 4,
        out_specs=(vmem, hbm, vmem),
        scratch_shapes=[
            pltpu.VMEM((N, hidden_units), BF16),
            pltpu.VMEM((N, width), BF16),
            pltpu.VMEM((1, LANES), F32),
            pltpu.VMEM((E, width // N), BF16),
            pltpu.VMEM((hidden_units, width), BF16),
            pltpu.SemaphoreType.DMA((4,)),
        ],
        compiler_params=pltpu.CompilerParams(vmem_limit_bytes=32 * 1024 * 1024),
    )(hidden, grads, loss, grad_router)
    return loss.reshape(()), grad_down, grad_router.T


def solution(mesh):
    sizes = (mesh.shape["dp"], mesh.shape["seq"], mesh.shape["expert"])
    return jax.shard_map(
        functools.partial(shards, sizes),
        mesh=mesh,
        in_specs=(
            P("expert", ("dp", "seq"), None),
            P("expert", ("dp", "seq"), None),
            P("expert", ("dp", "seq"), None),
            P("expert", ("dp", "seq"), None),
            P(("dp", "seq"), None),
            P(),
            P(),
            P(("dp", "expert"), None, "seq"),
            P(("dp", "expert"), None, "seq"),
            P(("dp", "expert"), "seq", None),
            P(),
            P("expert", "dp", None),
            P("expert", None),
            P("expert", ("dp", "seq")),
            P("expert", None),
        ),
        out_specs=(P(), P(("dp", "expert"), "seq", None), P(("dp", "seq", "expert"), None)),
        check_vma=False,
    )
```

time: 45.8 us -> 45.2 us (0.987)
  matrix products: 2.66 us -> 0 us
  local copies, waits for them, and re-layouts: 0.6 us -> 2.93 us
  Pallas kernels: 39.5 us -> 40.7 us
  between operations: 2.49 us -> 1.3 us
    dot_general x1 -> x0, matrix products: 2.66 us -> none  [shards(): lax.dot_general(hidden, grads, (((0,), (0,)), ((), ())), preferred_elemen...]
    unnamed x5 -> x8, local copies, waits for them, and re-layouts: 0.6 us -> 2.93 us
    pallas_call x1 -> x2, Pallas kernels: 39.5 us -> 40.7 us  [the longest x1 38.5 us: shards(): pl.pallas_call(functools.partial(kernel, sizes, names), out_shape=tuple(o...]
where the time goes in v2:
time: 45.2 us; the launch traced here: 44.9 us
  Pallas kernels  40.7 us (90%)
  local copies, waits for them, and re-layouts  2.93 us (6%)
  between operations  1.3 us (3%)
    pallas_call x1, Pallas kernels, shards(): pl.pallas_call(functools.partial(kernel, sizes, names), out_shape=tuple(o...  38.5 us
    unnamed x8, local copies, waits for them, and re-layouts  2.93 us
    pallas_call x1, Pallas kernels, shards(): pl.pallas_call(down_kernel, out_shape=(jax.ShapeDtypeStruct((1, 1), F32),...  2.23 us

profile of v2, /device:TPU:1, one launch (start us, length us, event | category | flops | bytes accessed | tf_op | source)
XLA Modules:
  0.0 44.9 jit_solution(8627710786310463829)
XLA Ops:
  1.3 38.5 %shard_map.166 = (f32[1,128]{1,0:T(1,128)}, bf16[32,384]{1,0:T(8,128)(2,1)}, bf16[32,2048]{1,0:T(8,128)(2,1)}, bf16[16,64]{1,0:T(8,128)(2,1)}) custom-call(bf16[1,4096]{1,0:T(2,128)(2,1)} %bitcast.9, s32[1,8]{1,0:T(1,128)} %refs_1_.1, s32[1,8]{1,0:T(1,128)} %refs_2_.1, bf16[1,128,512]{2,1,0:T(8,128)(2,1)} %refs_3_.1, bf16[1,128,512]{2,1,0:T(8,128)(2,1)} %refs_4_.1, ...), custom_call_target="tpu_custom_call" | custom-call | tf_op jit(solution)/shard_map/pallas_call | solution.py:506
  39.8 0.0 copy-start
  39.8 0.9 %copy-done = bf16[32,2048]{1,0:T(8,128)(2,1)S(1)} copy-done((bf16[32,2048]{1,0:T(8,128)(2,1)S(1)}, bf16[32,2048]{1,0:T(8,128)(2,1)}, u32[]{:S(2)}) %copy-start) | copy-done | bytes 131096
  40.7 0.0 copy-start.1
  40.7 0.7 %copy-done.1 = bf16[32,384]{1,0:T(8,128)(2,1)S(1)} copy-done((bf16[32,384]{1,0:T(8,128)(2,1)S(1)}, bf16[32,384]{1,0:T(8,128)(2,1)}, u32[]{:S(2)}) %copy-start.1) | copy-done | bytes 24600
  41.4 0.0 copy-start.2
  41.4 0.7 %copy-done.2 = bf16[16,64]{1,0:T(8,128)(2,1)S(1)} copy-done((bf16[16,64]{1,0:T(8,128)(2,1)S(1)}, bf16[16,64]{1,0:T(8,128)(2,1)}, u32[]{:S(2)}) %copy-start.2) | copy-done | bytes 2072
  42.1 0.0 copy-start.3
  42.1 0.6 %copy-done.3 = f32[1,128]{1,0:T(1,128)S(1)} copy-done((f32[1,128]{1,0:T(1,128)S(1)}, f32[1,128]{1,0:T(1,128)}, u32[]{:S(2)}) %copy-start.3) | copy-done | bytes 536
  42.7 2.2 %shard_map.167 = (f32[1,1]{1,0:T(1,128)}, bf16[1,384,2048]{2,1,0:T(8,128)(2,1)}, bf16[16,64]{1,0:T(8,128)(2,1)}) custom-call(bf16[32,384]{1,0:T(8,128)(2,1)S(1)} %copy-done.1, bf16[32,2048]{1,0:T(8,128)(2,1)S(1)} %copy-done, f32[1,128]{1,0:T(1,128)S(1)} %copy-done.3, bf16[16,64]{1,0:T(8,128)(2,1)S(1)} %copy-done.2), custom_call_target="tpu_custom_call" | custom-call | tf_op jit(solution)/shard_map/pallas_call | solution.py:516
Async XLA Ops:
  39.8 0.9 %copy-start = (bf16[32,2048]{1,0:T(8,128)(2,1)S(1)}, bf16[32,2048]{1,0:T(8,128)(2,1)}, u32[]{:S(2)}) copy-start(bf16[32,2048]{1,0:T(8,128)(2,1)} %get-tuple-element.11.refs_1_) | copy-start | bytes 393220
  40.7 0.7 %copy-start.1 = (bf16[32,384]{1,0:T(8,128)(2,1)S(1)}, bf16[32,384]{1,0:T(8,128)(2,1)}, u32[]{:S(2)}) copy-start(bf16[32,384]{1,0:T(8,128)(2,1)} %get-tuple-element.10.refs_0_) | copy-start | bytes 73732
  41.4 0.7 %copy-start.2 = (bf16[16,64]{1,0:T(8,128)(2,1)S(1)}, bf16[16,64]{1,0:T(8,128)(2,1)}, u32[]{:S(2)}) copy-start(bf16[16,64]{1,0:T(8,128)(2,1)} %get-tuple-element.13.refs_3_) | copy-start | bytes 6148
  42.1 0.6 %copy-start.3 = (f32[1,128]{1,0:T(1,128)S(1)}, f32[1,128]{1,0:T(1,128)}, u32[]{:S(2)}) copy-start(f32[1,128]{1,0:T(1,128)} %get-tuple-element.12.refs_2_) | copy-start | bytes 1540

commit v3 on v2

--- a/solution.py
+++ b/solution.py
@@ -112,20 +112,15 @@
     def to_pack(body):
         each(1, G, lambda i: body(near(i // SQ, i % SQ, 0)))
 
-    def to_plane(body):
-        each(1, E, lambda i: body(near(i // EN, 0, i % EN)))
-
-    def to_pair(body):
-        each(1, SQ, lambda i: body(near(0, i, 0)))
+    def to_all(body):
+        each(1, N, lambda i: body(near(i // (SQ * EN), (i // EN) % SQ, i % EN)))
 
     barrier = pltpu.get_barrier_semaphore()
 
     def greet(to):
         pl.semaphore_signal(barrier, inc=1, device_id=to, device_id_type=MESH)
 
-    to_pack(greet)
-    each(1, EN, lambda c: each(0, DP, lambda a: greet(near(a, 0, c))))
-    partners = G - 1 + (EN - 1) * DP
+    to_all(greet)
 
     def send(source, target, number, to):
         pltpu.make_async_remote_copy(
@@ -147,7 +142,7 @@
     q_own[...] = jnp.concatenate(
         [q_row[:, h * LANES : (h + 1) * LANES] for h in range(QUERY_HEADS)], axis=0
     ).astype(BF16)
-    pl.semaphore_wait(barrier, partners)
+    pl.semaphore_wait(barrier, N - 1)
 
     to_pack(lambda to: send(q_own, q_buf.at[mine], 0, to))
     q_buf[mine] = q_own[...]
@@ -253,9 +248,8 @@
     norm_own, norm_buf, norm_f32, rows = r["norm_own"], r["norm_buf"], r["norm_f32"], r["rows"]
     norm_own[...] = normed
 
-    to_plane(lambda to: send(norm_own, norm_buf.at[me], 3, to))
+    to_all(lambda to: send(norm_own, norm_buf.at[me], 3, to))
     norm_buf[me] = norm_own[...]
-    plane = pl.ds(sq * E, E)
 
     normed = normed.astype(F32)
     logits = jnp.zeros((E, LANES), F32)
@@ -273,11 +267,9 @@
     )
     gate_weight = power / jnp.sum(power, axis=0, keepdims=True)
 
-    await_all(norm_buf, E - 1, recv_sem.at[3])
-    to_pair(lambda to: send(norm_buf.at[plane], norm_buf.at[plane], 4, to))
     for name in ("w_gate", "w_up", "w_down"):
         loads[name].wait()
-    await_all(norm_buf, N - E, recv_sem.at[4])
+    await_all(norm_buf, N - 1, recv_sem.at[3])
 
     norm_f32[...] = norm_buf[...].astype(F32).reshape(N * WB, LANES)
     for c in range(WB):
@@ -289,25 +281,23 @@
     stores = [pltpu.make_async_copy(r["hidden"], r["out_hidden"], load_sem.at[0])]
     stores[0].start()
     expert_out = jnp.dot(hidden, down_v[...], preferred_element_type=F32)
-    out_f32, half_send, half_buf = r["out_f32"], r["half_send"], r["half_buf"]
-    out_send, out_buf = r["out_send"], r["out_buf"]
+    out_f32, out_send, out_buf = r["out_f32"], r["out_send"], r["out_buf"]
     for c in range(WB):
         out_f32[pl.ds(c, N, stride=WB), :] = expert_out[:, c * LANES : (c + 1) * LANES]
-    half_send[...] = out_f32[...].astype(BF16).reshape(SQ, E, WB, LANES)
-
-    to_pair(lambda to: send(half_send.at[to[1]], half_buf.at[sq], 5, to))
-    await_all(half_buf, SQ - 1, recv_sem.at[5])
-    outs = out_f32[pl.ds(pl.multiple_of(sq * (E * WB), E * WB), E * WB), :].reshape(E, WB, LANES)
-    for i in range(1, SQ):
-        outs += half_buf[lax.rem(sq + i, SQ)].astype(F32)
-    out_send[...] = outs.astype(BF16)
-    to_plane(lambda to: send(out_send.at[to[0] * EN + to[2]], out_buf.at[expert], 6, to))
-    out_buf[expert] = out_send[expert]
+    out_send[...] = out_f32[...].astype(BF16).reshape(N, WB, LANES)
+
+    def row_of(to):
+        return to[1] * E + to[0] * EN + to[2]
+
+    to_all(lambda to: send(out_send.at[row_of(to)], out_buf.at[me], 4, to))
+    out_buf[me] = out_send[me]
     own_label = r["labels"][...].astype(F32)
     weight_column = gate_weight.reshape(E, 1, 1)
-    await_all(out_buf, E - 1, recv_sem.at[6])
-
-    outs = out_buf[...].astype(F32)
+    await_all(out_buf, N - 1, recv_sem.at[4])
+
+    outs = out_buf[0:E].astype(F32)
+    for half in range(1, SQ):
+        outs += out_buf[half * E : (half + 1) * E].astype(F32)
     final = stream + jnp.sum(outs * weight_column, axis=0)
     scale = lax.rsqrt(total(final * final) * (1.0 / width) + EPSILON)
     along = total(final * head_f32)
@@ -322,7 +312,7 @@
     dlog_own, dlog_buf = r["dlog_own"], r["dlog_buf"]
     grad_send[...] = (weight_column * d_mix[None]).astype(BF16)
 
-    to_plane(lambda to: send(grad_send.at[to[0] * EN + to[2]], grad_buf.at[me], 7, to))
+    to_all(lambda to: send(grad_send.at[to[0] * EN + to[2]], grad_buf.at[me], 5, to))
     grad_buf[me] = grad_send[expert]
     route_dot = jnp.sum(jnp.sum(outs * d_mix[None], axis=1), axis=1, keepdims=True)
     mean_dot = jnp.sum(gate_weight * route_dot, axis=0, keepdims=True)
@@ -332,18 +322,14 @@
     dlog_own[...] = jnp.concatenate(
         [d_logits, jnp.broadcast_to(row_loss, (1, LANES))], axis=0
     )
-    to_plane(lambda to: send(dlog_own, dlog_buf.at[me], 9, to))
+    to_all(lambda to: send(dlog_own, dlog_buf.at[me], 6, to))
     dlog_buf[me] = dlog_own[...]
     share = width // N
     first = (mine * EN + ex) * share
     own_columns = norm_f32[pl.ds(first // LANES, N, stride=WB), :]
     own_columns = pltpu.roll(own_columns, lax.rem(LANES - lax.rem(first, LANES), LANES), 1)
 
-    await_all(grad_buf, E - 1, recv_sem.at[7])
-    to_pair(lambda to: send(grad_buf.at[plane], grad_buf.at[plane], 8, to))
-    await_all(dlog_buf, E - 1, recv_sem.at[9])
-    to_pair(lambda to: send(dlog_buf.at[plane], dlog_buf.at[plane], 10, to))
-    await_all(grad_buf, N - E, recv_sem.at[8])
+    await_all(grad_buf, N - 1, recv_sem.at[5])
     grad_f32[...] = grad_buf[...].astype(F32).reshape(N * WB, LANES)
     for c in range(WB):
         r["grads"][:, c * LANES : (c + 1) * LANES] = grad_f32[
@@ -351,7 +337,7 @@
         ].astype(BF16)
     stores.append(pltpu.make_async_copy(r["grads"], r["out_grads"], load_sem.at[1]))
     stores[-1].start()
-    await_all(dlog_buf, N - E, recv_sem.at[10])
+    await_all(dlog_buf, N - 1, recv_sem.at[6])
     r["loss"][...] = jnp.sum(dlog_buf[:, 1, :], axis=0, keepdims=True)
     router_grad = lax.dot_general(
         dlog_buf[:, 0, :],
@@ -371,14 +357,10 @@
             (q_buf, G - 1),
             (part_buf, G - 1),
             (mix_buf, G - 1),
-            (norm_buf, E - 1),
-            (norm_buf, N - E),
-            (half_buf, SQ - 1),
-            (out_buf, E - 1),
-            (grad_buf, E - 1),
-            (grad_buf, N - E),
-            (dlog_buf, E - 1),
-            (dlog_buf, N - E),
+            (norm_buf, N - 1),
+            (out_buf, N - 1),
+            (grad_buf, N - 1),
+            (dlog_buf, N - 1),
         ]
     ):
         await_all(buf, count, send_sem.at[number])
@@ -489,18 +471,16 @@
         norm_f32=pltpu.VMEM((N * WB, LANES), F32),
         rows=pltpu.VMEM((N, width), BF16),
         out_f32=pltpu.VMEM((N * WB, LANES), F32),
-        half_send=pltpu.VMEM((SQ, E) + message, BF16),
-        half_buf=pltpu.VMEM((SQ, E) + message, BF16),
-        out_send=pltpu.VMEM((E,) + message, BF16),
-        out_buf=pltpu.VMEM((E,) + message, BF16),
+        out_send=pltpu.VMEM((N,) + message, BF16),
+        out_buf=pltpu.VMEM((N,) + message, BF16),
         grad_send=pltpu.VMEM((E,) + message, BF16),
         grad_buf=pltpu.VMEM((N,) + message, BF16),
         grad_f32=pltpu.VMEM((N * WB, LANES), F32),
         dlog_own=pltpu.VMEM((2, LANES), F32),
         dlog_buf=pltpu.VMEM((N, 2, LANES), F32),
         load_sem=pltpu.SemaphoreType.DMA((len(INPUTS),)),
-        send_sem=pltpu.SemaphoreType.DMA((11,)),
-        recv_sem=pltpu.SemaphoreType.DMA((11,)),
+        send_sem=pltpu.SemaphoreType.DMA((7,)),
+        recv_sem=pltpu.SemaphoreType.DMA((7,)),
     )
     names = ["in_" + name for name in INPUTS] + list(outs) + list(scratch)
     loss, hidden, grads, grad_router = pl.pallas_call(
@@ -530,7 +510,7 @@
             pltpu.VMEM((hidden_units, width), BF16),
             pltpu.SemaphoreType.DMA((4,)),
         ],
-        compiler_params=pltpu.CompilerParams(vmem_limit_bytes=32 * 1024 * 1024),
+        compiler_params=pltpu.CompilerParams(vmem_limit_bytes=60 * 1024 * 1024),
     )(hidden, grads, loss, grad_router)
     return loss.reshape(()), grad_down, grad_router.T
 

time: 45.2 us -> 43 us (0.951)
  local copies, waits for them, and re-layouts: 2.93 us -> 0 us
    unnamed x8 -> x0, local copies, waits for them, and re-layouts: 2.93 us -> none
    pallas_call x1, Pallas kernels: 2.23 us -> 2.97 us  [shards(): pl.pallas_call(down_kernel, out_shape=(jax.ShapeDtypeStruct((1, 1), F32),...]
where the time goes in v3:
time: 43 us; the launch traced here: 42.4 us
  Pallas kernels  41.1 us (96%)
  between operations  1.29 us (3%)
    pallas_call x1, Pallas kernels, shards(): pl.pallas_call(functools.partial(kernel, sizes, names), out_shape=tuple(o...  38.1 us
    pallas_call x1, Pallas kernels, shards(): pl.pallas_call(down_kernel, out_shape=(jax.ShapeDtypeStruct((1, 1), F32),...  2.97 us

profile of v3, /device:TPU:1, one launch (start us, length us, event | category | flops | bytes accessed | tf_op | source)
XLA Modules:
  0.0 42.4 jit_solution(14312882480540035787)
XLA Ops:
  1.3 38.1 %shard_map.166 = (f32[1,128]{1,0:T(1,128)}, bf16[32,384]{1,0:T(8,128)(2,1)}, bf16[32,2048]{1,0:T(8,128)(2,1)}, bf16[16,64]{1,0:T(8,128)(2,1)}) custom-call(bf16[1,4096]{1,0:T(2,128)(2,1)} %bitcast.9, s32[1,8]{1,0:T(1,128)} %refs_1_.1, s32[1,8]{1,0:T(1,128)} %refs_2_.1, bf16[1,128,512]{2,1,0:T(8,128)(2,1)} %refs_3_.1, bf16[1,128,512]{2,1,0:T(8,128)(2,1)} %refs_4_.1, ...), custom_call_target="tpu_custom_call" | custom-call | tf_op jit(solution)/shard_map/pallas_call | solution.py:486
  39.4 3.0 %shard_map.167 = (f32[1,1]{1,0:T(1,128)}, bf16[1,384,2048]{2,1,0:T(8,128)(2,1)}, bf16[16,64]{1,0:T(8,128)(2,1)}) custom-call(bf16[32,384]{1,0:T(8,128)(2,1)} %get-tuple-element.10.refs_0_, bf16[32,2048]{1,0:T(8,128)(2,1)} %get-tuple-element.11.refs_1_, f32[1,128]{1,0:T(1,128)} %get-tuple-element.12.refs_2_, bf16[16,64]{1,0:T(8,128)(2,1)} %get-tuple-element.13.refs_3_), custom_call_target="tpu_custom_call" | custom-call | tf_op jit(solution)/shard_map/pallas_call | solution.py:496

commit v4 on v2

--- a/solution.py
+++ b/solution.py
@@ -31,6 +31,7 @@
     "w_up",
     "w_down",
 )
+LARGE = ("out_proj", "w_gate", "w_up", "w_down")
 MESH = pl.DeviceIdType.MESH
 F32 = jnp.float32
 BF16 = jnp.bfloat16
@@ -72,8 +73,8 @@
     WB = width // LANES
     dp, sq, ex = lax.axis_index("dp"), lax.axis_index("seq"), lax.axis_index("expert")
     mine = dp * SQ + sq
-    expert = dp * EN + ex
-    me = sq * E + expert
+    block = sq * E + ex * DP
+    me = block + dp
     tokens = r["keys"].shape[0]
     load_sem, send_sem, recv_sem = r["load_sem"], r["send_sem"], r["recv_sem"]
 
@@ -83,7 +84,8 @@
         if len(source.shape) > len(target.shape):
             source = source.at[0]
         loads[name] = pltpu.make_async_copy(source, target, load_sem.at[i])
-        loads[name].start()
+        if name not in LARGE:
+            loads[name].start()
 
     if unroll:
         near_dp = [lax.rem(dp + a, DP) for a in range(DP)]
@@ -112,8 +114,11 @@
     def to_pack(body):
         each(1, G, lambda i: body(near(i // SQ, i % SQ, 0)))
 
-    def to_plane(body):
-        each(1, E, lambda i: body(near(i // EN, 0, i % EN)))
+    def along_dp(body):
+        each(1, DP, lambda i: body(near(i, 0, 0)))
+
+    def along_expert(body):
+        each(1, EN, lambda i: body(near(0, 0, i)))
 
     def to_pair(body):
         each(1, SQ, lambda i: body(near(0, i, 0)))
@@ -124,8 +129,8 @@
         pl.semaphore_signal(barrier, inc=1, device_id=to, device_id_type=MESH)
 
     to_pack(greet)
-    each(1, EN, lambda c: each(0, DP, lambda a: greet(near(a, 0, c))))
-    partners = G - 1 + (EN - 1) * DP
+    along_expert(greet)
+    partners = G - 1 + EN - 1
 
     def send(source, target, number, to):
         pltpu.make_async_remote_copy(
@@ -150,10 +155,12 @@
     pl.semaphore_wait(barrier, partners)
 
     to_pack(lambda to: send(q_own, q_buf.at[mine], 0, to))
+    for name in LARGE:
+        loads[name].start()
     q_buf[mine] = q_own[...]
 
     for name in INPUTS:
-        if name not in ("queries", "out_proj", "w_gate", "w_up", "w_down"):
+        if name != "queries" and name not in LARGE:
             loads[name].wait()
     traces = r["trace_len"].shape[1]
     pos_col = to_column(r["step_pos"][...].astype(F32), G)
@@ -253,9 +260,12 @@
     norm_own, norm_buf, norm_f32, rows = r["norm_own"], r["norm_buf"], r["norm_f32"], r["rows"]
     norm_own[...] = normed
 
-    to_plane(lambda to: send(norm_own, norm_buf.at[me], 3, to))
+    line, plane = pl.ds(block, DP), pl.ds(sq * E, E)
+    along_dp(lambda to: send(norm_own, norm_buf.at[me], 3, to))
     norm_buf[me] = norm_own[...]
-    plane = pl.ds(sq * E, E)
+
+    await_all(norm_buf, DP - 1, recv_sem.at[3])
+    along_expert(lambda to: send(norm_buf.at[line], norm_buf.at[line], 4, to))
 
     normed = normed.astype(F32)
     logits = jnp.zeros((E, LANES), F32)
@@ -273,11 +283,11 @@
     )
     gate_weight = power / jnp.sum(power, axis=0, keepdims=True)
 
-    await_all(norm_buf, E - 1, recv_sem.at[3])
-    to_pair(lambda to: send(norm_buf.at[plane], norm_buf.at[plane], 4, to))
+    await_all(norm_buf, E - DP, recv_sem.at[4])
+    to_pair(lambda to: send(norm_buf.at[plane], norm_buf.at[plane], 5, to))
     for name in ("w_gate", "w_up", "w_down"):
         loads[name].wait()
-    await_all(norm_buf, N - E, recv_sem.at[4])
+    await_all(norm_buf, N - E, recv_sem.at[5])
 
     norm_f32[...] = norm_buf[...].astype(F32).reshape(N * WB, LANES)
     for c in range(WB):
@@ -295,19 +305,24 @@
         out_f32[pl.ds(c, N, stride=WB), :] = expert_out[:, c * LANES : (c + 1) * LANES]
     half_send[...] = out_f32[...].astype(BF16).reshape(SQ, E, WB, LANES)
 
-    to_pair(lambda to: send(half_send.at[to[1]], half_buf.at[sq], 5, to))
-    await_all(half_buf, SQ - 1, recv_sem.at[5])
+    to_pair(lambda to: send(half_send.at[to[1]], half_buf.at[sq], 6, to))
+    await_all(half_buf, SQ - 1, recv_sem.at[6])
     outs = out_f32[pl.ds(pl.multiple_of(sq * (E * WB), E * WB), E * WB), :].reshape(E, WB, LANES)
     for i in range(1, SQ):
         outs += half_buf[lax.rem(sq + i, SQ)].astype(F32)
-    out_send[...] = outs.astype(BF16)
-    to_plane(lambda to: send(out_send.at[to[0] * EN + to[2]], out_buf.at[expert], 6, to))
-    out_buf[expert] = out_send[expert]
+    out_send[...] = outs.astype(BF16).reshape(EN, DP, WB, LANES)
+    out_mid = r["out_mid"]
+    along_expert(lambda to: send(out_send.at[to[2]], out_mid.at[ex], 7, to))
+    out_mid[ex] = out_send[ex]
+    await_all(out_mid, EN - 1, recv_sem.at[7])
+    along_dp(lambda to: send(out_mid.at[:, to[0]], out_buf.at[dp], 8, to))
+    for c in range(EN):
+        out_buf[dp, c] = out_mid[c, dp]
     own_label = r["labels"][...].astype(F32)
     weight_column = gate_weight.reshape(E, 1, 1)
-    await_all(out_buf, E - 1, recv_sem.at[6])
-
-    outs = out_buf[...].astype(F32)
+    await_all(out_buf, DP - 1, recv_sem.at[8])
+
+    outs = out_buf[...].astype(F32).reshape(E, WB, LANES)
     final = stream + jnp.sum(outs * weight_column, axis=0)
     scale = lax.rsqrt(total(final * final) * (1.0 / width) + EPSILON)
     along = total(final * head_f32)
@@ -320,10 +335,11 @@
     ).astype(BF16).astype(F32)
     grad_send, grad_buf, grad_f32 = r["grad_send"], r["grad_buf"], r["grad_f32"]
     dlog_own, dlog_buf = r["dlog_own"], r["dlog_buf"]
-    grad_send[...] = (weight_column * d_mix[None]).astype(BF16)
-
-    to_plane(lambda to: send(grad_send.at[to[0] * EN + to[2]], grad_buf.at[me], 7, to))
-    grad_buf[me] = grad_send[expert]
+    grad_send[...] = (weight_column * d_mix[None]).astype(BF16).reshape(DP, EN, WB, LANES)
+
+    grad_mid = r["grad_mid"]
+    along_dp(lambda to: send(grad_send.at[to[0]], grad_mid.at[dp], 9, to))
+    grad_mid[dp] = grad_send[dp]
     route_dot = jnp.sum(jnp.sum(outs * d_mix[None], axis=1), axis=1, keepdims=True)
     mean_dot = jnp.sum(gate_weight * route_dot, axis=0, keepdims=True)
     d_logits = to_row(gate_weight * (route_dot - mean_dot), E)
@@ -332,18 +348,24 @@
     dlog_own[...] = jnp.concatenate(
         [d_logits, jnp.broadcast_to(row_loss, (1, LANES))], axis=0
     )
-    to_plane(lambda to: send(dlog_own, dlog_buf.at[me], 9, to))
+    along_dp(lambda to: send(dlog_own, dlog_buf.at[me], 12, to))
     dlog_buf[me] = dlog_own[...]
+    await_all(grad_mid, DP - 1, recv_sem.at[9])
+    along_expert(lambda to: send(grad_mid.at[:, to[2]], grad_buf.at[line], 10, to))
+    for a in range(DP):
+        grad_buf[block + a] = grad_mid[a, ex]
+    await_all(dlog_buf, DP - 1, recv_sem.at[12])
+    along_expert(lambda to: send(dlog_buf.at[line], dlog_buf.at[line], 13, to))
     share = width // N
     first = (mine * EN + ex) * share
     own_columns = norm_f32[pl.ds(first // LANES, N, stride=WB), :]
     own_columns = pltpu.roll(own_columns, lax.rem(LANES - lax.rem(first, LANES), LANES), 1)
 
-    await_all(grad_buf, E - 1, recv_sem.at[7])
-    to_pair(lambda to: send(grad_buf.at[plane], grad_buf.at[plane], 8, to))
-    await_all(dlog_buf, E - 1, recv_sem.at[9])
-    to_pair(lambda to: send(dlog_buf.at[plane], dlog_buf.at[plane], 10, to))
-    await_all(grad_buf, N - E, recv_sem.at[8])
+    await_all(grad_buf, E - DP, recv_sem.at[10])
+    to_pair(lambda to: send(grad_buf.at[plane], grad_buf.at[plane], 11, to))
+    await_all(dlog_buf, E - DP, recv_sem.at[13])
+    to_pair(lambda to: send(dlog_buf.at[plane], dlog_buf.at[plane], 14, to))
+    await_all(grad_buf, N - E, recv_sem.at[11])
     grad_f32[...] = grad_buf[...].astype(F32).reshape(N * WB, LANES)
     for c in range(WB):
         r["grads"][:, c * LANES : (c + 1) * LANES] = grad_f32[
@@ -351,7 +373,7 @@
         ].astype(BF16)
     stores.append(pltpu.make_async_copy(r["grads"], r["out_grads"], load_sem.at[1]))
     stores[-1].start()
-    await_all(dlog_buf, N - E, recv_sem.at[10])
+    await_all(dlog_buf, N - E, recv_sem.at[14])
     r["loss"][...] = jnp.sum(dlog_buf[:, 1, :], axis=0, keepdims=True)
     router_grad = lax.dot_general(
         dlog_buf[:, 0, :],
@@ -371,13 +393,17 @@
             (q_buf, G - 1),
             (part_buf, G - 1),
             (mix_buf, G - 1),
-            (norm_buf, E - 1),
+            (norm_buf, DP - 1),
+            (norm_buf, E - DP),
             (norm_buf, N - E),
             (half_buf, SQ - 1),
-            (out_buf, E - 1),
-            (grad_buf, E - 1),
+            (out_mid, EN - 1),
+            (out_buf, DP - 1),
+            (grad_mid, DP - 1),
+            (grad_buf, E - DP),
             (grad_buf, N - E),
-            (dlog_buf, E - 1),
+            (dlog_buf, DP - 1),
+            (dlog_buf, E - DP),
             (dlog_buf, N - E),
         ]
     ):
@@ -491,16 +517,18 @@
         out_f32=pltpu.VMEM((N * WB, LANES), F32),
         half_send=pltpu.VMEM((SQ, E) + message, BF16),
         half_buf=pltpu.VMEM((SQ, E) + message, BF16),
-        out_send=pltpu.VMEM((E,) + message, BF16),
-        out_buf=pltpu.VMEM((E,) + message, BF16),
-        grad_send=pltpu.VMEM((E,) + message, BF16),
+        out_send=pltpu.VMEM((EN, DP) + message, BF16),
+        out_mid=pltpu.VMEM((EN, DP) + message, BF16),
+        out_buf=pltpu.VMEM((DP, EN) + message, BF16),
+        grad_send=pltpu.VMEM((DP, EN) + message, BF16),
+        grad_mid=pltpu.VMEM((DP, EN) + message, BF16),
         grad_buf=pltpu.VMEM((N,) + message, BF16),
         grad_f32=pltpu.VMEM((N * WB, LANES), F32),
         dlog_own=pltpu.VMEM((2, LANES), F32),
         dlog_buf=pltpu.VMEM((N, 2, LANES), F32),
         load_sem=pltpu.SemaphoreType.DMA((len(INPUTS),)),
-        send_sem=pltpu.SemaphoreType.DMA((11,)),
-        recv_sem=pltpu.SemaphoreType.DMA((11,)),
+        send_sem=pltpu.SemaphoreType.DMA((15,)),
+        recv_sem=pltpu.SemaphoreType.DMA((15,)),
     )
     names = ["in_" + name for name in INPUTS] + list(outs) + list(scratch)
     loss, hidden, grads, grad_router = pl.pallas_call(
@@ -530,7 +558,7 @@
             pltpu.VMEM((hidden_units, width), BF16),
             pltpu.SemaphoreType.DMA((4,)),
         ],
-        compiler_params=pltpu.CompilerParams(vmem_limit_bytes=32 * 1024 * 1024),
+        compiler_params=pltpu.CompilerParams(vmem_limit_bytes=60 * 1024 * 1024),
     )(hidden, grads, loss, grad_router)
     return loss.reshape(()), grad_down, grad_router.T
 

time: 45.2 us -> 50 us (1.11)
  Pallas kernels: 40.7 us -> 48.5 us
  local copies, waits for them, and re-layouts: 2.93 us -> 0 us
    pallas_call x1, Pallas kernels: 38.5 us -> 45.5 us  [shards(): pl.pallas_call(functools.partial(kernel, sizes, names), out_shape=tuple(o...]
    unnamed x8 -> x0, local copies, waits for them, and re-layouts: 2.93 us -> none
    pallas_call x1, Pallas kernels: 2.23 us -> 2.97 us  [shards(): pl.pallas_call(down_kernel, out_shape=(jax.ShapeDtypeStruct((1, 1), F32),...]
where the time goes in v4:
time: 50 us; the launch traced here: 49.8 us
  Pallas kernels  48.5 us (97%)
  between operations  1.29 us (3%)
    pallas_call x1, Pallas kernels, shards(): pl.pallas_call(functools.partial(kernel, sizes, names), out_shape=tuple(o...  45.5 us
    pallas_call x1, Pallas kernels, shards(): pl.pallas_call(down_kernel, out_shape=(jax.ShapeDtypeStruct((1, 1), F32),...  2.97 us

profile of v4, /device:TPU:1, one launch (start us, length us, event | category | flops | bytes accessed | tf_op | source)
XLA Modules:
  0.0 49.8 jit_solution(14881380979289349263)
XLA Ops:
  1.3 45.5 %shard_map.166 = (f32[1,128]{1,0:T(1,128)}, bf16[32,384]{1,0:T(8,128)(2,1)}, bf16[32,2048]{1,0:T(8,128)(2,1)}, bf16[16,64]{1,0:T(8,128)(2,1)}) custom-call(bf16[1,4096]{1,0:T(2,128)(2,1)} %bitcast.9, s32[1,8]{1,0:T(1,128)} %refs_1_.1, s32[1,8]{1,0:T(1,128)} %refs_2_.1, bf16[1,128,512]{2,1,0:T(8,128)(2,1)} %refs_3_.1, bf16[1,128,512]{2,1,0:T(8,128)(2,1)} %refs_4_.1, ...), custom_call_target="tpu_custom_call" | custom-call | tf_op jit(solution)/shard_map/pallas_call | solution.py:534
  46.8 3.0 %shard_map.167 = (f32[1,1]{1,0:T(1,128)}, bf16[1,384,2048]{2,1,0:T(8,128)(2,1)}, bf16[16,64]{1,0:T(8,128)(2,1)}) custom-call(bf16[32,384]{1,0:T(8,128)(2,1)} %get-tuple-element.10.refs_0_, bf16[32,2048]{1,0:T(8,128)(2,1)} %get-tuple-element.11.refs_1_, f32[1,128]{1,0:T(1,128)} %get-tuple-element.12.refs_2_, bf16[16,64]{1,0:T(8,128)(2,1)} %get-tuple-element.13.refs_3_), custom_call_target="tpu_custom_call" | custom-call | tf_op jit(solution)/shard_map/pallas_call | solution.py:544

commit v5 on v2

--- a/solution.py
+++ b/solution.py
@@ -1,4 +1,5 @@
 import functools
+import itertools
 
 import jax
 import jax.numpy as jnp
@@ -97,6 +98,8 @@
         def near(a, b, c):
             return lax.rem(dp + a, DP), lax.rem(sq + b, SQ), lax.rem(ex + c, EN)
 
+    far_first = sorted(range(DP), key=lambda a: abs(a - DP // 2))
+
     def each(first, last, body):
         if unroll:
             for i in range(first, last):
@@ -110,10 +113,20 @@
             lax.fori_loop(first, last, step, 0)
 
     def to_pack(body):
-        each(1, G, lambda i: body(near(i // SQ, i % SQ, 0)))
+        if unroll:
+            for a, b in itertools.product(far_first, range(SQ)):
+                if a or b:
+                    body(near(a, b, 0))
+        else:
+            each(1, G, lambda i: body(near(i // SQ, i % SQ, 0)))
 
     def to_plane(body):
-        each(1, E, lambda i: body(near(i // EN, 0, i % EN)))
+        if unroll:
+            for a, c in itertools.product(far_first, range(EN)):
+                if a or c:
+                    body(near(a, 0, c))
+        else:
+            each(1, E, lambda i: body(near(i // EN, 0, i % EN)))
 
     def to_pair(body):
         each(1, SQ, lambda i: body(near(0, i, 0)))
@@ -214,21 +227,15 @@
     pick = lane == lax.rem(mine, per_block) * QUERY_HEADS + iota((QUERY_HEADS, LANES), 0)
     await_all(part_buf, G - 1, recv_sem.at[1])
 
-    peak_of, sum_of = [], []
+    stats = [part_buf[s, QUERY_HEADS:].astype(F32) for s in range(G)]
+    peak_rows = jnp.concatenate([t[0:1] + t[1:2] + t[2:3] for t in stats], axis=0)
+    sum_rows = jnp.concatenate([t[3:4] + t[4:5] + t[5:6] for t in stats], axis=0)
+    factors = jnp.exp(peak_rows - jnp.max(peak_rows, axis=0, keepdims=True))
+    factors = factors / jnp.sum(sum_rows * factors, axis=0, keepdims=True)
+    attn = jnp.zeros((QUERY_HEADS, LANES), F32)
     for s in range(G):
-        stat = part_buf[s, QUERY_HEADS:].astype(F32)
-        peak_row = stat[0:1] + stat[1:2] + stat[2:3]
-        sum_row = stat[3:4] + stat[4:5] + stat[5:6]
-        peak_of.append(jnp.sum(jnp.where(pick, peak_row, 0.0), axis=1, keepdims=True))
-        sum_of.append(jnp.sum(jnp.where(pick, sum_row, 0.0), axis=1, keepdims=True))
-    peak_all = functools.reduce(jnp.maximum, peak_of)
-    weighted = jnp.zeros((QUERY_HEADS, LANES), F32)
-    sum_all = jnp.zeros((QUERY_HEADS, 1), F32)
-    for s in range(G):
-        factor = jnp.exp(peak_of[s] - peak_all)
-        weighted += part_buf[s, 0:QUERY_HEADS].astype(F32) * factor
-        sum_all += sum_of[s] * factor
-    attn = weighted / sum_all
+        factor = jnp.sum(jnp.where(pick, factors[s : s + 1], 0.0), axis=1, keepdims=True)
+        attn += part_buf[s, 0:QUERY_HEADS].astype(F32) * factor
     attn = jnp.concatenate(
         [attn[h * G : (h + 1) * G] for h in range(QUERY_HEADS // G)], axis=1
     ).astype(BF16)
@@ -386,36 +393,37 @@
         store.wait()
 
 
-def down_kernel(*refs):
-    sources, (loss_out, down_out, router_out), targets = refs[:4], refs[4:7], refs[7:11]
-    stage, sem = refs[11:]
+def down_kernel(
+    hidden, grads, loss, router_grad, loss_out, down_out, router_out, rows, columns, stage, sem
+):
     loads = [
-        pltpu.make_async_copy(source, target, sem.at[i])
-        for i, (source, target) in enumerate(zip(sources, targets))
+        pltpu.make_async_copy(hidden, rows, sem.at[4]),
+        pltpu.make_async_copy(grads, columns, sem.at[5]),
     ]
-    for load in loads:
-        load.start()
+    passes = [
+        pltpu.make_async_copy(loss, loss_out, sem.at[6]),
+        pltpu.make_async_copy(router_grad, router_out, sem.at[7]),
+    ]
+    for copy in loads + passes:
+        copy.start()
     for load in loads:
         load.wait()
-    hidden, grads, loss, router_grad = targets
     step = stage.shape[1] // 4
     stores = []
     for i in range(4):
-        columns = pl.ds(i * step, step)
+        span = pl.ds(i * step, step)
         stage[:, i * step : (i + 1) * step] = lax.dot_general(
-            hidden[...],
-            grads[:, i * step : (i + 1) * step],
+            rows[...],
+            columns[:, i * step : (i + 1) * step],
             (((0,), (0,)), ((), ())),
             preferred_element_type=F32,
         ).astype(BF16)
         stores.append(
-            pltpu.make_async_copy(stage.at[:, columns], down_out.at[0, :, columns], sem.at[i])
+            pltpu.make_async_copy(stage.at[:, span], down_out.at[0, :, span], sem.at[i])
         )
         stores[-1].start()
-    loss_out[...] = loss[:, 0:1]
-    router_out[...] = router_grad[...]
-    for store in stores:
-        store.wait()
+    for copy in stores + passes:
+        copy.wait()
 
 
 def shards(
@@ -443,7 +451,6 @@
     WB = width // LANES
     hidden_units = w_gate.shape[2]
     hbm = pl.BlockSpec(memory_space=pl.ANY)
-    vmem = pl.BlockSpec(memory_space=pltpu.VMEM)
     message = (WB, LANES)
     operands = dict(
         queries=queries[0],
@@ -516,23 +523,21 @@
     loss, grad_down, grad_router = pl.pallas_call(
         down_kernel,
         out_shape=(
-            jax.ShapeDtypeStruct((1, 1), F32),
+            jax.ShapeDtypeStruct((1, LANES), F32),
             jax.ShapeDtypeStruct((1, hidden_units, width), BF16),
             jax.ShapeDtypeStruct((E, width // N), BF16),
         ),
         in_specs=[hbm] * 4,
-        out_specs=(vmem, hbm, vmem),
+        out_specs=(hbm, hbm, hbm),
         scratch_shapes=[
             pltpu.VMEM((N, hidden_units), BF16),
             pltpu.VMEM((N, width), BF16),
-            pltpu.VMEM((1, LANES), F32),
-            pltpu.VMEM((E, width // N), BF16),
             pltpu.VMEM((hidden_units, width), BF16),
-            pltpu.SemaphoreType.DMA((4,)),
+            pltpu.SemaphoreType.DMA((8,)),
         ],
-        compiler_params=pltpu.CompilerParams(vmem_limit_bytes=32 * 1024 * 1024),
+        compiler_params=pltpu.CompilerParams(vmem_limit_bytes=60 * 1024 * 1024),
     )(hidden, grads, loss, grad_router)
-    return loss.reshape(()), grad_down, grad_router.T
+    return loss[0, 0], grad_down, grad_router.T
 
 
 def solution(mesh):

time: 45.2 us -> 43 us (0.951)
  local copies, waits for them, and re-layouts: 2.93 us -> 0 us
  Pallas kernels: 40.7 us -> 41.5 us
    unnamed x8 -> x0, local copies, waits for them, and re-layouts: 2.93 us -> none
    pallas_call x1, Pallas kernels: 38.5 us -> 39.1 us  [shards(): pl.pallas_call(functools.partial(kernel, sizes, names), out_shape=tuple(o...]
where the time goes in v5:
time: 43 us; the launch traced here: 42.8 us
  Pallas kernels  41.5 us (97%)
  between operations  1.29 us (3%)
    pallas_call x1, Pallas kernels, shards(): pl.pallas_call(functools.partial(kernel, sizes, names), out_shape=tuple(o...  39.1 us
    pallas_call x1, Pallas kernels, shards(): pl.pallas_call(down_kernel, out_shape=(jax.ShapeDtypeStruct((1, LANES), F...  2.42 us

profile of v5, /device:TPU:1, one launch (start us, length us, event | category | flops | bytes accessed | tf_op | source)
XLA Modules:
  0.0 42.8 jit_solution(14415440468506333946)
XLA Ops:
  1.3 39.1 %shard_map.166 = (f32[1,128]{1,0:T(1,128)}, bf16[32,384]{1,0:T(8,128)(2,1)}, bf16[32,2048]{1,0:T(8,128)(2,1)}, bf16[16,64]{1,0:T(8,128)(2,1)}) custom-call(bf16[1,4096]{1,0:T(2,128)(2,1)} %bitcast.10, s32[1,8]{1,0:T(1,128)} %refs_1_.1, s32[1,8]{1,0:T(1,128)} %refs_2_.1, bf16[1,128,512]{2,1,0:T(8,128)(2,1)} %refs_3_.1, bf16[1,128,512]{2,1,0:T(8,128)(2,1)} %refs_4_.1, ...), custom_call_target="tpu_custom_call" | custom-call | tf_op jit(solution)/shard_map/pallas_call | solution.py:513
  40.4 2.4 %shard_map.167 = (f32[1,128]{1,0:T(1,128)}, bf16[1,384,2048]{2,1,0:T(8,128)(2,1)}, bf16[16,64]{1,0:T(8,128)(2,1)}) custom-call(bf16[32,384]{1,0:T(8,128)(2,1)} %get-tuple-element.10.hidden, bf16[32,2048]{1,0:T(8,128)(2,1)} %get-tuple-element.11.grads, f32[1,128]{1,0:T(1,128)} %get-tuple-element.12.loss, bf16[16,64]{1,0:T(8,128)(2,1)} %get-tuple-element.13.router_grad), custom_call_target="tpu_custom_call" | custom-call | tf_op jit(solution)/shard_map/pallas_call | solution.py:523

commit v6 on v5

--- a/solution.py
+++ b/solution.py
@@ -1,5 +1,4 @@
 import functools
-import itertools
 
 import jax
 import jax.numpy as jnp
@@ -98,8 +97,6 @@
         def near(a, b, c):
             return lax.rem(dp + a, DP), lax.rem(sq + b, SQ), lax.rem(ex + c, EN)
 
-    far_first = sorted(range(DP), key=lambda a: abs(a - DP // 2))
-
     def each(first, last, body):
         if unroll:
             for i in range(first, last):
@@ -113,20 +110,13 @@
             lax.fori_loop(first, last, step, 0)
 
     def to_pack(body):
-        if unroll:
-            for a, b in itertools.product(far_first, range(SQ)):
-                if a or b:
-                    body(near(a, b, 0))
-        else:
-            each(1, G, lambda i: body(near(i // SQ, i % SQ, 0)))
+        each(1, G, lambda i: body(near(i // SQ, i % SQ, 0)))
 
     def to_plane(body):
-        if unroll:
-            for a, c in itertools.product(far_first, range(EN)):
-                if a or c:
-                    body(near(a, 0, c))
-        else:
-            each(1, E, lambda i: body(near(i // EN, 0, i % EN)))
+        each(1, E, lambda i: body(near(i // EN, 0, i % EN)))
+
+    def to_all(body):
+        each(1, N, lambda i: body(near(i // (SQ * EN), (i // EN) % SQ, i % EN)))
 
     def to_pair(body):
         each(1, SQ, lambda i: body(near(0, i, 0)))
@@ -136,9 +126,7 @@
     def greet(to):
         pl.semaphore_signal(barrier, inc=1, device_id=to, device_id_type=MESH)
 
-    to_pack(greet)
-    each(1, EN, lambda c: each(0, DP, lambda a: greet(near(a, 0, c))))
-    partners = G - 1 + (EN - 1) * DP
+    to_all(greet)
 
     def send(source, target, number, to):
         pltpu.make_async_remote_copy(
@@ -160,7 +148,7 @@
     q_own[...] = jnp.concatenate(
         [q_row[:, h * LANES : (h + 1) * LANES] for h in range(QUERY_HEADS)], axis=0
     ).astype(BF16)
-    pl.semaphore_wait(barrier, partners)
+    pl.semaphore_wait(barrier, N - 1)
 
     to_pack(lambda to: send(q_own, q_buf.at[mine], 0, to))
     q_buf[mine] = q_own[...]
@@ -329,7 +317,7 @@
     dlog_own, dlog_buf = r["dlog_own"], r["dlog_buf"]
     grad_send[...] = (weight_column * d_mix[None]).astype(BF16)
 
-    to_plane(lambda to: send(grad_send.at[to[0] * EN + to[2]], grad_buf.at[me], 7, to))
+    to_all(lambda to: send(grad_send.at[to[0] * EN + to[2]], grad_buf.at[me], 7, to))
     grad_buf[me] = grad_send[expert]
     route_dot = jnp.sum(jnp.sum(outs * d_mix[None], axis=1), axis=1, keepdims=True)
     mean_dot = jnp.sum(gate_weight * route_dot, axis=0, keepdims=True)
@@ -339,18 +327,14 @@
     dlog_own[...] = jnp.concatenate(
         [d_logits, jnp.broadcast_to(row_loss, (1, LANES))], axis=0
     )
-    to_plane(lambda to: send(dlog_own, dlog_buf.at[me], 9, to))
+    to_all(lambda to: send(dlog_own, dlog_buf.at[me], 8, to))
     dlog_buf[me] = dlog_own[...]
     share = width // N
     first = (mine * EN + ex) * share
     own_columns = norm_f32[pl.ds(first // LANES, N, stride=WB), :]
     own_columns = pltpu.roll(own_columns, lax.rem(LANES - lax.rem(first, LANES), LANES), 1)
 
-    await_all(grad_buf, E - 1, recv_sem.at[7])
-    to_pair(lambda to: send(grad_buf.at[plane], grad_buf.at[plane], 8, to))
-    await_all(dlog_buf, E - 1, recv_sem.at[9])
-    to_pair(lambda to: send(dlog_buf.at[plane], dlog_buf.at[plane], 10, to))
-    await_all(grad_buf, N - E, recv_sem.at[8])
+    await_all(grad_buf, N - 1, recv_sem.at[7])
     grad_f32[...] = grad_buf[...].astype(F32).reshape(N * WB, LANES)
     for c in range(WB):
         r["grads"][:, c * LANES : (c + 1) * LANES] = grad_f32[
@@ -358,7 +342,7 @@
         ].astype(BF16)
     stores.append(pltpu.make_async_copy(r["grads"], r["out_grads"], load_sem.at[1]))
     stores[-1].start()
-    await_all(dlog_buf, N - E, recv_sem.at[10])
+    await_all(dlog_buf, N - 1, recv_sem.at[8])
     r["loss"][...] = jnp.sum(dlog_buf[:, 1, :], axis=0, keepdims=True)
     router_grad = lax.dot_general(
         dlog_buf[:, 0, :],
@@ -382,10 +366,8 @@
             (norm_buf, N - E),
             (half_buf, SQ - 1),
             (out_buf, E - 1),
-            (grad_buf, E - 1),
-            (grad_buf, N - E),
-            (dlog_buf, E - 1),
-            (dlog_buf, N - E),
+            (grad_buf, N - 1),
+            (dlog_buf, N - 1),
         ]
     ):
         await_all(buf, count, send_sem.at[number])
@@ -506,8 +488,8 @@
         dlog_own=pltpu.VMEM((2, LANES), F32),
         dlog_buf=pltpu.VMEM((N, 2, LANES), F32),
         load_sem=pltpu.SemaphoreType.DMA((len(INPUTS),)),
-        send_sem=pltpu.SemaphoreType.DMA((11,)),
-        recv_sem=pltpu.SemaphoreType.DMA((11,)),
+        send_sem=pltpu.SemaphoreType.DMA((9,)),
+        recv_sem=pltpu.SemaphoreType.DMA((9,)),
     )
     names = ["in_" + name for name in INPUTS] + list(outs) + list(scratch)
     loss, hidden, grads, grad_router = pl.pallas_call(

time: 43 us -> 42.2 us (0.981)
  Pallas kernels: 41.5 us -> 40.3 us
    pallas_call x1, Pallas kernels: 39.1 us -> 37.9 us  [shards(): pl.pallas_call(functools.partial(kernel, sizes, names), out_shape=tuple(o...]
where the time goes in v6:
time: 42.2 us; the launch traced here: 41.6 us
  Pallas kernels  40.3 us (95%)
  between operations  1.29 us (3%)
    pallas_call x1, Pallas kernels, shards(): pl.pallas_call(functools.partial(kernel, sizes, names), out_shape=tuple(o...  37.9 us
    pallas_call x1, Pallas kernels, shards(): pl.pallas_call(down_kernel, out_shape=(jax.ShapeDtypeStruct((1, LANES), F...  2.42 us

profile of v6, /device:TPU:1, one launch (start us, length us, event | category | flops | bytes accessed | tf_op | source)
XLA Modules:
  0.0 41.6 jit_solution(3434458909563161436)
XLA Ops:
  1.3 37.9 %shard_map.166 = (f32[1,128]{1,0:T(1,128)}, bf16[32,384]{1,0:T(8,128)(2,1)}, bf16[32,2048]{1,0:T(8,128)(2,1)}, bf16[16,64]{1,0:T(8,128)(2,1)}) custom-call(bf16[1,4096]{1,0:T(2,128)(2,1)} %bitcast.10, s32[1,8]{1,0:T(1,128)} %refs_1_.1, s32[1,8]{1,0:T(1,128)} %refs_2_.1, bf16[1,128,512]{2,1,0:T(8,128)(2,1)} %refs_3_.1, bf16[1,128,512]{2,1,0:T(8,128)(2,1)} %refs_4_.1, ...), custom_call_target="tpu_custom_call" | custom-call | tf_op jit(solution)/shard_map/pallas_call | solution.py:495
  39.2 2.4 %shard_map.167 = (f32[1,128]{1,0:T(1,128)}, bf16[1,384,2048]{2,1,0:T(8,128)(2,1)}, bf16[16,64]{1,0:T(8,128)(2,1)}) custom-call(bf16[32,384]{1,0:T(8,128)(2,1)} %get-tuple-element.10.hidden, bf16[32,2048]{1,0:T(8,128)(2,1)} %get-tuple-element.11.grads, f32[1,128]{1,0:T(1,128)} %get-tuple-element.12.loss, bf16[16,64]{1,0:T(8,128)(2,1)} %get-tuple-element.13.router_grad), custom_call_target="tpu_custom_call" | custom-call | tf_op jit(solution)/shard_map/pallas_call | solution.py:505
